TPU v7x, 512 devices: a whole 4x8x8 slice. The times are simulated.
512 devices in a mesh: dp: 16 (over y, core), cell: 32 (over z, x).
Axes of the slice: x: 4, y: 8, z: 8, core: 2. Of those that a mesh axis runs over, the one named last changes fastest.
Arguments:
- blocks: bfloat16 [16, 32, 8, 256, 256], P('dp', 'cell'), may hold values from -0.375 to 0.375
- row_block: int32 [16, 32, 8], P('dp', 'cell'), may hold values from 0 to 5, as said below
- col_block: int32 [16, 32, 8], P('dp', 'cell'), may hold values from 0 to 5
- counts: int32 [16, 32], P('dp', 'cell'), may hold values from 2 to 8, as said below
- observed: float32 [24576, 128], P(('dp', 'cell'))
Outputs:
- model: float32 [49152, 128], P(('cell', 'dp'))
- residual: float32 [24576, 128], P(('dp', 'cell'))
Inputs may be any that keep to these rules, and one draw needn't show every extreme that they name: Within one tile the slots name distinct positions (row_block, col_block); slots at or beyond the tile's count are ignored. `counts`: some tile has all 8 slots in use.
All inputs are finite; a program needn't handle non-finite values.
Results may differ from a plain program's by a relative error of at most 0.0057.
Values may be sent and summed in bfloat16 or wider, within the bound.
A program may use at most 64 MiB of HBM per device.

v0:
```python
import jax
import jax.numpy as jnp
from jax import lax
from jax.sharding import PartitionSpec as P

RB = 6
CB = 6
ITERS = 2


def shards(blocks, row_block, col_block, counts, observed):
    tiles = blocks[0, 0]
    rows_of = row_block[0, 0]
    cols_of = col_block[0, 0]
    used = counts[0, 0]
    width = tiles.shape[1]
    columns = observed.shape[1]
    tile_rows = RB * width
    tile_cols = CB * width

    def adjoint(vec_full):

        def adjoint_add_block(slot, total):
            piece = lax.dynamic_slice_in_dim(vec_full, rows_of[slot] * width, width, 0)
            term = lax.dot_general(
                tiles[slot], piece, (((0,), (0,)), ((), ())), preferred_element_type=jnp.float32
            )
            start = cols_of[slot] * width
            old = lax.dynamic_slice_in_dim(total, start, width, 0)
            return lax.dynamic_update_slice_in_dim(total, old + term, start, 0)

        return lax.fori_loop(
            0, used, adjoint_add_block, jnp.zeros((tile_cols, columns), jnp.float32)
        )

    def gradient_of(residual):
        whole = lax.all_gather(residual.astype(jnp.bfloat16), "cell", axis=0, tiled=True)
        return lax.psum_scatter(adjoint(whole), "dp", scatter_dimension=0, tiled=True)

    def squares(values):
        return lax.psum(jnp.sum(values * values, axis=0), ("dp", "cell"))

    residual = observed
    gradient = gradient_of(residual)
    model = jnp.zeros_like(gradient)
    direction = gradient
    gamma = squares(gradient)
    for step in range(ITERS):
        image_whole = lax.all_gather(direction.astype(jnp.bfloat16), "dp", axis=0, tiled=True)
        forward_vec_full = image_whole

        def forward_add_block(slot, total):
            piece = lax.dynamic_slice_in_dim(forward_vec_full, cols_of[slot] * width, width, 0)
            term = jnp.dot(tiles[slot], piece, preferred_element_type=jnp.float32)
            start = rows_of[slot] * width
            old = lax.dynamic_slice_in_dim(total, start, width, 0)
            return lax.dynamic_update_slice_in_dim(total, old + term, start, 0)

        image = lax.psum_scatter(
            lax.fori_loop(0, used, forward_add_block, jnp.zeros((tile_rows, columns), jnp.float32)),
            "cell",
            scatter_dimension=0,
            tiled=True,
        )
        alpha = gamma / squares(image)
        model = model + alpha * direction
        residual = residual - alpha * image
        if step + 1 < ITERS:
            gradient = gradient_of(residual)
            gamma_new = squares(gradient)
            direction = gradient + gamma_new / gamma * direction
            gamma = gamma_new
    return (model, residual)


def solution(mesh):
    in_specs = (
        P("dp", "cell", None, None, None),
        P("dp", "cell", None),
        P("dp", "cell", None),
        P("dp", "cell"),
        P(("dp", "cell"), None),
    )
    out_specs = (P(("cell", "dp"), None), P(("dp", "cell"), None))
    return jax.shard_map(shards, mesh=mesh, in_specs=in_specs, out_specs=out_specs, check_vma=False)
```

profile of v0, /device:TPU:1, one launch (start us, length us, event | category | flops | bytes accessed | tf_op | source)
XLA Modules:
  0.0 1102.6 jit_solution(3857274847736749113)
XLA Ops:
  7.2 0.0 reduce-scatter.5.cloned.1.call-start
  7.2 0.8 convert_element_type.12
  8.0 44.2 %all_gather.12 = bf16[1536,128]{1,0:T(8,128)(2,1)S(1)} all-gather(bf16[48,128]{1,0:T(8,128)(2,1)S(1)} %convert_element_type.12), channel_id=1, replica_groups=mesh['dp'=16,'cell'=32] {'cell'}, dimensions={0}, use_global_device_ids=true | all-gather | bytes 405504 | tf_op jit(solution)/shard_map/all_gather | solution.py:37
  52.3 0.1 broadcast.6.clone
  52.3 0.6 copy-done.9
  52.9 7.4 while.40
  53.6 0.6 dynamic_slice.112
  54.8 0.6 dynamic_slice.111
  56.1 0.2 fusion.36
  57.0 0.6 dynamic_slice.112
  58.2 0.6 dynamic_slice.111
  59.5 0.2 fusion.36
  60.4 0.9 copy-done.2
  61.3 0.0 reduce-scatter.5.cloned.1.call-update
  61.3 0.0 reduce-scatter.7.cloned.1.call-start
  61.3 85.8 %reduce-scatter.5.cloned.1.call-done = f32[96,128]{1,0:T(8,128)} async-done(((f32[1536,128]{1,0:T(8,128)}), f32[96,128]{1,0:T(8,128)}) %reduce-scatter.5.cloned.1.call-update) | async-done | bytes 49168 | tf_op jit(solution)/shard_map/reduce_scatter | solution.py:38
  147.2 0.9 multiply_reduce_fusion.1
  148.1 17.5 %all_gather.13 = bf16[1536,128]{1,0:T(8,128)(2,1)S(1)} all-gather(bf16[96,128]{1,0:T(8,128)(2,1)S(1)} %get-tuple-element.217), channel_id=1, replica_groups=mesh['dp'=16,'cell'=32] {'dp'}, dimensions={0}, use_global_device_ids=true | all-gather | bytes 417792 | tf_op jit(solution)/shard_map/all_gather | solution.py:49
  165.6 0.1 broadcast.6.clone.2
  165.6 7.3 while.41
  166.3 0.6 dynamic_slice.117
  167.5 0.6 dynamic_slice.116
  168.8 0.2 fusion.39
  169.6 0.6 dynamic_slice.117
  170.9 0.6 dynamic_slice.116
  172.1 0.2 fusion.39
  173.0 0.9 copy-done.3
  173.8 0.0 reduce-scatter.7.cloned.1.call-update
  173.9 0.0 reduce-scatter.9.cloned.1.call-start
  173.9 232.2 %reduce-scatter.7.cloned.1.call-done = f32[48,128]{1,0:T(8,128)} async-done(((f32[1536,128]{1,0:T(8,128)}), f32[48,128]{1,0:T(8,128)}) %reduce-scatter.7.cloned.1.call-update) | async-done | bytes 24592 | tf_op jit(solution)/shard_map/reduce_scatter | solution.py:59
  406.1 0.8 multiply_reduce_fusion.3
  406.8 101.1 %all-reduce = (f32[128]{0:T(128)S(1)}, f32[128]{0:T(128)S(1)}) all-reduce(f32[128]{0:T(128)S(1)} %get-tuple-element.216, f32[128]{0:T(128)S(1)} %multiply_reduce_fusion.3), channel_id=1, replica_groups=mesh['dp'=16,'cell'=32] {'dp','cell'}, use_global_device_ids=true, to_apply=%region_4.0 | all-reduce | flops 256 | bytes 2048 | tf_op jit(solution)/shard_map/psum | solution.py:41
  507.9 0.7 fusion.21
  508.7 35.0 %all_gather.14 = bf16[1536,128]{1,0:T(8,128)(2,1)S(1)} all-gather(bf16[48,128]{1,0:T(8,128)(2,1)S(1)} %fusion.21), channel_id=1, replica_groups=mesh['dp'=16,'cell'=32] {'cell'}, dimensions={0}, use_global_device_ids=true | all-gather | bytes 405504 | tf_op jit(solution)/shard_map/all_gather | solution.py:37
  543.7 0.1 broadcast.6.clone.1
  543.7 7.4 while.42
  544.4 0.6 dynamic_slice.122
  545.7 0.6 dynamic_slice.121
  546.9 0.2 fusion.42
  547.8 0.6 dynamic_slice.122
  549.0 0.6 dynamic_slice.121
  550.3 0.2 fusion.42
  551.2 0.9 copy-done.4
  552.1 0.0 reduce-scatter.11.cloned.1.call-start
  552.2 85.2 %reduce-scatter.9.cloned.1.call-done = f32[96,128]{1,0:T(8,128)} async-done(((f32[1536,128]{1,0:T(8,128)}), f32[96,128]{1,0:T(8,128)}) %reduce-scatter.9.cloned.1.call-update) | async-done | bytes 49168 | tf_op jit(solution)/shard_map/reduce_scatter | solution.py:38
  637.4 0.8 multiply_reduce_fusion
  638.2 99.8 %psum.30 = f32[128]{0:T(128)S(1)} all-reduce(f32[128]{0:T(128)S(1)} %multiply_reduce_fusion), channel_id=1, replica_groups=mesh['dp'=16,'cell'=32] {'dp','cell'}, use_global_device_ids=true, to_apply=%region_14.0 | all-reduce | flops 128 | bytes 1024 | tf_op jit(solution)/shard_map/psum | solution.py:41
  738.0 0.8 fusion.20
  738.8 17.2 %all_gather.15 = bf16[1536,128]{1,0:T(8,128)(2,1)S(1)} all-gather(bf16[96,128]{1,0:T(8,128)(2,1)S(1)} %fusion.20), channel_id=1, replica_groups=mesh['dp'=16,'cell'=32] {'dp'}, dimensions={0}, use_global_device_ids=true | all-gather | bytes 417792 | tf_op jit(solution)/shard_map/all_gather | solution.py:49
  756.0 0.1 broadcast.6
  756.0 7.3 while.43
  756.7 0.6 dynamic_slice.127
  757.9 0.6 dynamic_slice.126
  759.2 0.2 fusion.45
  760.0 0.6 dynamic_slice.127
  761.3 0.6 dynamic_slice.126
  762.5 0.2 fusion.45
  763.4 0.9 copy-done.1
  764.2 0.0 reduce-scatter.11.cloned.1.call-update
  764.3 228.6 %reduce-scatter.11.cloned.1.call-done = f32[48,128]{1,0:T(8,128)} async-done(((f32[1536,128]{1,0:T(8,128)}), f32[48,128]{1,0:T(8,128)}) %reduce-scatter.11.cloned.1.call-update) | async-done | bytes 24592 | tf_op jit(solution)/shard_map/reduce_scatter | solution.py:59
  992.9 0.8 multiply_reduce_fusion.2
  993.6 100.5 %psum.31 = f32[128]{0:T(128)S(1)} all-reduce(f32[128]{0:T(128)S(1)} %multiply_reduce_fusion.2), channel_id=1, replica_groups=mesh['dp'=16,'cell'=32] {'dp','cell'}, use_global_device_ids=true, to_apply=%region_19.0 | all-reduce | flops 128 | bytes 1024 | tf_op jit(solution)/shard_map/psum | solution.py:41
  1094.1 1.4 multiply_subtract_fusion
  1095.5 0.6 multiply_add_fusion
  (21 shorter events, 0.1 us)
Async XLA Ops:
  7.2 45.2 %copy-start = (bf16[1,1,8,256,256]{4,3,2,1,0:T(8,128)(2,1)S(1)}, bf16[1,1,8,256,256]{4,3,2,1,0:T(8,128)(2,1)}, u32[]{:S(2)}) copy-start(bf16[1,1,8,256,256]{4,3,2,1,0:T(8,128)(2,1)} %param.13) | copy-start | bytes 3145732
  7.2 140.0 %reduce-scatter.5.cloned.1.call-start = ((), (), s32[]{:S(2)}) async-start(), calls=%async_computation.4 | async-start | bytes 835584 | tf_op jit(solution)/shard_map/reduce_scatter | solution.py:38
  52.3 0.7 copy-start.9
  52.3 0.7 copy-start.10
  60.4 0.9 copy-start.2
  61.3 344.8 %reduce-scatter.7.cloned.1.call-start = ((), (), s32[]{:S(2)}) async-start(), calls=%async_computation.5 | async-start | bytes 811008 | tf_op jit(solution)/shard_map/reduce_scatter | solution.py:59
  173.0 0.9 copy-start.3
  173.9 334.1 %copy-start.7 = (f32[48,128]{1,0:T(8,128)S(1)}, f32[48,128]{1,0:T(8,128)}, u32[]{:S(2)}) copy-start(f32[48,128]{1,0:T(8,128)} %param.17) | copy-start | bytes 73732
  173.9 463.5 %reduce-scatter.9.cloned.1.call-start = ((), (), s32[]{:S(2)}) async-start(), calls=%async_computation.6 | async-start | bytes 835584 | tf_op jit(solution)/shard_map/reduce_scatter | solution.py:38
  551.2 0.9 copy-start.4
  552.1 185.9 %copy-start.5 = (f32[96,128]{1,0:T(8,128)S(1)}, f32[96,128]{1,0:T(8,128)}, u32[]{:S(2)}) copy-start(f32[96,128]{1,0:T(8,128)} %reduce-scatter.5.cloned.1.call-done) | copy-start | bytes 147460
  552.1 440.8 %reduce-scatter.11.cloned.1.call-start = ((), (), s32[]{:S(2)}) async-start(), calls=%async_computation.7 | async-start | bytes 811008 | tf_op jit(solution)/shard_map/reduce_scatter | solution.py:59
  763.4 0.9 copy-start.1
  764.3 329.8 %copy-start.8 = (f32[48,128]{1,0:T(8,128)S(1)}, f32[48,128]{1,0:T(8,128)}, u32[]{:S(2)}) copy-start(f32[48,128]{1,0:T(8,128)} %reduce-scatter.7.cloned.1.call-done) | copy-start | bytes 73732
  1094.1 1.4 copy-start.6
Sparse Core Ops, SparseCore 0:
  61.4 85.7 reduce-scatter.4
  174.0 232.0 reduce-scatter.6
  552.2 85.1 reduce-scatter.8
  764.4 228.4 reduce-scatter.10
where the time goes:
time: 1100 us
  waiting for transfers between devices  632 us (57%)
  blocking collectives  415 us (38%)
  loops' own time  18.5 us (2%)
  between operations  13.9 us (1%)
  local copies, waits for them, and re-layouts  13.7 us (1%)
    reduce_scatter x2, waiting for transfers between devices, shards(): lax.psum_scatter(lax.fori_loop(0, used, forward_add_block, jnp.zeros((til...  461 us
    psum x3, blocking collectives, squares(): return lax.psum(jnp.sum(values * values, axis=0), ('dp', 'cell'))  301 us
    reduce_scatter x2, waiting for transfers between devices, gradient_of(): lax.psum_scatter(adjoint(whole), 'dp', scatter_dimension=0, tiled=True)  171 us
    all_gather x2, blocking collectives, gradient_of(): lax.all_gather(residual.astype(jnp.bfloat16), 'cell', axis=0, tiled=True)  79.2 us
    all_gather x2, blocking collectives, shards(): lax.all_gather(direction.astype(jnp.bfloat16), 'dp', axis=0, tiled=True)  34.6 us
  transfers between devices with their start and end apart: 4, of which 4 were waited for; matrix products, arithmetic and copies ran while one was open for 0% of the time, Pallas kernels for 0%

commit v1 on v0

v1 whole, which is shorter than its diff:
```python
import jax
import jax.numpy as jnp
from jax import lax
from jax.experimental import pallas as pl
from jax.experimental.pallas import tpu as pltpu
from jax.sharding import PartitionSpec as P

F32 = jnp.float32
BF16 = jnp.bfloat16
MESH = pl.DeviceIdType.MESH
SLOTS = 8
BLOCK = 256
NY = 8
NZ = 8
NX = 4
N_DP = NY * 2
N_CELL = NZ * NX
TILE = 6 * BLOCK
DROWS = TILE // N_CELL
CROWS = TILE // N_DP
COLS = 128


def far_first(i, n):
    return jnp.where(i % 2 == 1, n // 2 - (i + 1) // 2, n // 2 + i // 2)


def rows_at(ref, index, size):
    return ref.at[pl.ds(pl.multiple_of(index * size, size), size)]


def cgls(
    tiles,
    row_of,
    col_of,
    counts,
    observed,
    model_out,
    residual_out,
    tiles_t,
    pieces,
    prod,
    residual_full,
    image_full,
    direction_full,
    grad_send,
    pair_recv,
    grad_pair,
    grad_recv,
    image_send,
    image_recv,
    gamma_part,
    gamma_recv,
    delta_part,
    delta_recv,
    delta_dp_part,
    delta_cell,
    last_dp_part,
    last_dp,
    last_cell_part,
    last_cell,
    gather_send_sem,
    gather_recv_sem,
    dir_send_sem,
    dir_recv_sem,
    fwd_send_sem,
    fwd_recv_sem,
    pair_send_sem,
    pair_recv_sem,
    grad_send_sem,
    grad_recv_sem,
    image_send_sem,
    image_recv_sem,
    small_send_sem,
    small_recv_sem,
):
    dp = lax.axis_index("dp")
    cell = lax.axis_index("cell")
    y, core = dp // 2, dp % 2
    z, x = cell // NX, cell % NX
    sibling = (y * 2 + 1 - core, cell)

    def cell_peer(i):
        dz = far_first(i // NX, NZ)
        dx = far_first(i % NX, NX)
        return ((z + dz) % NZ) * NX + (x + dx) % NX

    def y_peer(i):
        return (y + far_first(i, NY)) % NY

    def dp_peer(i):
        return y_peer(i // 2) * 2 + (core + 1 + i) % 2

    def over_cells(step):
        lax.fori_loop(0, N_CELL - 1, lambda i, c: (step(cell_peer(i)), c)[1], 0)

    def over_dp(step):
        lax.fori_loop(0, N_DP - 1, lambda i, c: (step(dp_peer(i)), c)[1], 0)

    def over_y(step):
        lax.fori_loop(0, NY - 1, lambda i, c: (step(y_peer(i)), c)[1], 0)

    def remote(src, dst, send, recv, device):
        return pltpu.make_async_remote_copy(
            src_ref=src, dst_ref=dst, send_sem=send, recv_sem=recv, device_id=device, device_id_type=MESH
        )

    def wait_bytes(ref, sem):
        pltpu.make_async_copy(ref, ref, sem).wait()

    barrier = pltpu.get_barrier_semaphore()
    over_cells(lambda p: pl.semaphore_signal(barrier, inc=1, device_id=(dp, p), device_id_type=MESH))
    over_dp(lambda p: pl.semaphore_signal(barrier, inc=1, device_id=(p, cell), device_id_type=MESH))
    pl.semaphore_wait(barrier, N_CELL + N_DP - 2)

    used = counts[0, 0]

    def apply(matrix, source, target, vector, send):
        def multiply(slot, carry):
            prod[slot] = jnp.dot(matrix[slot], pieces[source[0, 0, slot]], preferred_element_type=F32)
            return carry

        for at in range(6):
            pieces[at] = vector[pl.ds(at * BLOCK, BLOCK), :]
        lax.fori_loop(0, SLOTS, multiply, 0)

        def place(at, carry):
            total = jnp.zeros((BLOCK, COLS), F32)
            for slot in range(SLOTS):
                here = jnp.logical_and(target[0, 0, slot] == at, slot < used)
                total = total + here.astype(F32) * prod[slot]
            send[pl.ds(pl.multiple_of(at * BLOCK, BLOCK), BLOCK), :] = total.astype(send.dtype)
            return carry

        lax.fori_loop(0, 6, place, 0)

    def gather_cells(full, k):
        mine = rows_at(full, cell, DROWS)
        over_cells(lambda p: remote(mine, mine, gather_send_sem.at[k], gather_recv_sem.at[k], (dp, p)).start())

    def gather_cells_wait(full, k):
        others = full.at[pl.ds(0, (N_CELL - 1) * DROWS)]
        wait_bytes(others, gather_recv_sem.at[k])
        wait_bytes(others, gather_send_sem.at[k])

    def gather_dp(full, k):
        mine = rows_at(full, dp, CROWS)
        over_y(lambda p: remote(mine, mine, dir_send_sem.at[k], dir_recv_sem.at[k, y], (p * 2 + core, cell)).start())
        remote(mine, mine, fwd_send_sem.at[k], fwd_recv_sem.at[k], sibling).start()

        def forward(i, carry):
            src = y_peer(NY - 2 - i)
            slot = rows_at(full, src * 2 + core, CROWS)
            wait_bytes(slot, dir_recv_sem.at[k, src])
            remote(slot, slot, fwd_send_sem.at[k], fwd_recv_sem.at[k], sibling).start()
            return carry

        lax.fori_loop(0, NY - 1, forward, 0)
        wait_bytes(full.at[pl.ds(0, NY * CROWS)], fwd_recv_sem.at[k])
        wait_bytes(full.at[pl.ds(0, NY * CROWS)], fwd_send_sem.at[k])
        wait_bytes(full.at[pl.ds(0, (NY - 1) * CROWS)], dir_send_sem.at[k])

    def scatter_dp(k):
        def pair(i, carry):
            src = rows_at(grad_send.at[k], i * 2 + 1 - core, CROWS)
            remote(src, rows_at(pair_recv.at[k], i, CROWS), pair_send_sem.at[k], pair_recv_sem.at[k], sibling).start()
            return carry

        lax.fori_loop(0, NY, pair, 0)
        wait_bytes(pair_recv.at[k], pair_recv_sem.at[k])

        def add(i, carry):
            at = far_first(i, NY)
            at = (y + at) % NY
            kept = grad_send[k, pl.ds(pl.multiple_of((at * 2 + core) * CROWS, CROWS), CROWS), :]
            got = pair_recv[k, pl.ds(pl.multiple_of(at * CROWS, CROWS), CROWS), :]
            grad_pair[k, pl.ds(pl.multiple_of(at * CROWS, CROWS), CROWS), :] = (kept + got).astype(BF16)
            return carry

        lax.fori_loop(0, NY, add, 0)
        slot = rows_at(grad_recv.at[k], y, CROWS)
        over_y(
            lambda p: remote(
                rows_at(grad_pair.at[k], p, CROWS), slot, grad_send_sem.at[k], grad_recv_sem.at[k], (p * 2 + core, cell)
            ).start()
        )
        grad_recv[k, pl.ds(pl.multiple_of(y * CROWS, CROWS), CROWS), :] = grad_pair[
            k, pl.ds(pl.multiple_of(y * CROWS, CROWS), CROWS), :
        ]

    def scatter_dp_wait(k):
        others = grad_recv.at[k, pl.ds(0, (NY - 1) * CROWS)]
        wait_bytes(others, grad_recv_sem.at[k])
        wait_bytes(others, grad_send_sem.at[k])
        wait_bytes(pair_recv.at[k], pair_send_sem.at[k])
        total = jnp.zeros((CROWS, COLS), F32)
        for i in range(NY):
            total = total + grad_recv[k, pl.ds(i * CROWS, CROWS), :].astype(F32)
        return total

    def scatter_cells(k):
        slot = rows_at(image_recv.at[k], cell, DROWS)

        def send(p):
            remote(
                rows_at(image_send.at[k], p, DROWS), slot, image_send_sem.at[k], image_recv_sem.at[k], (dp, p)
            ).start()

        over_cells(send)
        mine = pl.ds(pl.multiple_of(cell * DROWS, DROWS), DROWS)
        image_recv[k, mine, :] = image_send[k, mine, :]

    def scatter_cells_wait(k):
        others = image_recv.at[k, pl.ds(0, (N_CELL - 1) * DROWS)]
        wait_bytes(others, image_recv_sem.at[k])
        wait_bytes(others, image_send_sem.at[k])

        def add(i, total):
            return total + image_recv[k, pl.ds(pl.multiple_of(i * DROWS, DROWS), DROWS), :].astype(F32)

        return lax.fori_loop(0, N_CELL, add, jnp.zeros((DROWS, COLS), F32))

    def squares(full):
        def add(i, total):
            part = full[pl.ds(pl.multiple_of(i * 128, 128), 128), :].astype(F32)
            return total + part * part

        return jnp.sum(lax.fori_loop(0, TILE // 128, add, jnp.zeros((128, COLS), F32)), axis=0, keepdims=True)

    def small_over_cells(part, recv, k):
        recv[cell] = part[...]
        over_cells(
            lambda p: remote(part, recv.at[cell], small_send_sem.at[k], small_recv_sem.at[k], (dp, p)).start()
        )

    def small_over_dp(part, recv, k):
        recv[dp] = part[...]
        over_dp(lambda p: remote(part, recv.at[dp], small_send_sem.at[k], small_recv_sem.at[k], (p, cell)).start())

    def small_wait(recv, k, n):
        wait_bytes(recv.at[pl.ds(0, n - 1)], small_recv_sem.at[k])
        wait_bytes(recv.at[pl.ds(0, n - 1)], small_send_sem.at[k])
        return jnp.sum(recv[...], axis=0)

    residual_full[pl.ds(pl.multiple_of(cell * DROWS, DROWS), DROWS), :] = observed[...].astype(BF16)
    gather_cells(residual_full, 0)
    for slot in range(SLOTS):
        tiles_t[slot] = tiles[slot].T
    gather_cells_wait(residual_full, 0)

    apply(tiles_t, row_of, col_of, residual_full, grad_send.at[0])
    scatter_dp(0)
    gradient = scatter_dp_wait(0)
    model_out[...] = gradient
    my_cells = pl.ds(pl.multiple_of(dp * CROWS, CROWS), CROWS)
    my_rows = pl.ds(pl.multiple_of(cell * DROWS, DROWS), DROWS)

    direction_full[0, my_cells, :] = gradient.astype(BF16)
    gather_dp(direction_full.at[0], 0)
    apply(tiles, col_of, row_of, direction_full.at[0], image_send.at[0])
    scatter_cells(0)
    gamma_part[0] = squares(direction_full.at[0])
    small_over_cells(gamma_part.at[0], gamma_recv.at[0], 0)
    image = scatter_cells_wait(0)
    residual_out[...] = image
    gamma = small_wait(gamma_recv.at[0], 0, N_CELL)

    delta_part[...] = jnp.sum(image * image, axis=0, keepdims=True)
    small_over_dp(delta_part, delta_recv, 1)
    delta_dp_part[...] = small_wait(delta_recv, 1, N_DP)
    small_over_cells(delta_dp_part, delta_cell, 5)
    alpha = gamma / small_wait(delta_cell, 5, N_CELL)
    residual = observed[...] - alpha * image

    image_full[my_rows, :] = residual.astype(BF16)
    gather_cells(image_full, 1)
    gather_cells_wait(image_full, 1)
    apply(tiles_t, row_of, col_of, image_full, grad_send.at[1])
    scatter_dp(1)
    gradient = scatter_dp_wait(1)
    first = model_out[...]

    direction_full[1, my_cells, :] = gradient.astype(BF16)
    gather_dp(direction_full.at[1], 1)
    apply(tiles, col_of, row_of, direction_full.at[1], image_send.at[1])
    scatter_cells(1)
    gamma_part[1] = squares(direction_full.at[1])
    small_over_cells(gamma_part.at[1], gamma_recv.at[1], 2)
    image_one = scatter_cells_wait(1)
    gamma_one = small_wait(gamma_recv.at[1], 2, N_CELL)
    beta = gamma_one / gamma
    image_zero = residual_out[...]
    image_one = image_one + beta * image_zero

    last_dp_part[...] = jnp.sum(image_one * image_one, axis=0, keepdims=True)
    small_over_dp(last_dp_part, last_dp, 3)
    direction = gradient + beta * first
    model = alpha * first
    last_cell_part[...] = small_wait(last_dp, 3, N_DP)
    small_over_cells(last_cell_part, last_cell, 4)
    delta_one = small_wait(last_cell, 4, N_CELL)
    alpha_one = gamma_one / delta_one
    model_out[...] = model + alpha_one * direction
    residual_out[...] = residual - alpha_one * image_one


def shards(blocks, row_block, col_block, counts, observed):
    vmem = pl.BlockSpec(memory_space=pltpu.VMEM)
    smem = pl.BlockSpec(memory_space=pltpu.SMEM)
    dma = pltpu.SemaphoreType.DMA
    return pl.pallas_call(
        cgls,
        out_shape=(
            jax.ShapeDtypeStruct((CROWS, COLS), F32),
            jax.ShapeDtypeStruct((DROWS, COLS), F32),
        ),
        in_specs=[vmem, smem, smem, smem, vmem],
        out_specs=(vmem, vmem),
        scratch_shapes=[
            pltpu.VMEM((SLOTS, BLOCK, BLOCK), BF16),
            pltpu.VMEM((6, BLOCK, COLS), BF16),
            pltpu.VMEM((SLOTS, BLOCK, COLS), F32),
            pltpu.VMEM((TILE, COLS), BF16),
            pltpu.VMEM((TILE, COLS), BF16),
            pltpu.VMEM((2, TILE, COLS), BF16),
            pltpu.VMEM((2, TILE, COLS), F32),
            pltpu.VMEM((2, TILE // 2, COLS), F32),
            pltpu.VMEM((2, TILE // 2, COLS), BF16),
            pltpu.VMEM((2, TILE // 2, COLS), BF16),
            pltpu.VMEM((2, TILE, COLS), BF16),
            pltpu.VMEM((2, TILE, COLS), BF16),
            pltpu.VMEM((2, 1, COLS), F32),
            pltpu.VMEM((2, N_CELL, 1, COLS), F32),
            pltpu.VMEM((1, COLS), F32),
            pltpu.VMEM((N_DP, 1, COLS), F32),
            pltpu.VMEM((1, COLS), F32),
            pltpu.VMEM((N_CELL, 1, COLS), F32),
            pltpu.VMEM((1, COLS), F32),
            pltpu.VMEM((N_DP, 1, COLS), F32),
            pltpu.VMEM((1, COLS), F32),
            pltpu.VMEM((N_CELL, 1, COLS), F32),
            dma((2,)),
            dma((2,)),
            dma((2,)),
            dma((2, NY)),
            dma((2,)),
            dma((2,)),
            dma((2,)),
            dma((2,)),
            dma((2,)),
            dma((2,)),
            dma((2,)),
            dma((2,)),
            dma((6,)),
            dma((6,)),
        ],
        compiler_params=pltpu.CompilerParams(
            collective_id=0, has_side_effects=True, vmem_limit_bytes=40 * 1024 * 1024
        ),
        name="cgls",
    )(blocks[0, 0], row_block, col_block, counts, observed)


def solution(mesh):
    in_specs = (
        P("dp", "cell", None, None, None),
        P("dp", "cell", None),
        P("dp", "cell", None),
        P("dp", "cell"),
        P(("dp", "cell"), None),
    )
    out_specs = (P(("cell", "dp"), None), P(("dp", "cell"), None))
    return jax.shard_map(shards, mesh=mesh, in_specs=in_specs, out_specs=out_specs, check_vma=False)
```

time: 1100 us -> 133 us (0.12)
  waiting for transfers between devices: 632 us -> 0 us
  blocking collectives: 415 us -> 0 us
  Pallas kernels: 0 us -> 128 us
  loops' own time: 18.5 us -> 0 us
  between operations: 13.9 us -> 1.3 us
    reduce_scatter x4 -> x0, waiting for transfers between devices: 632 us -> none  [the longest x2 461 us: shards(): lax.psum_scatter(lax.fori_loop(0, used, forward_add_block, jnp.zeros((til...]
    psum x3 -> x0, blocking collectives: 301 us -> none  [squares(): return lax.psum(jnp.sum(values * values, axis=0), ('dp', 'cell'))]
    pallas_call x0 -> x1, Pallas kernels: none -> 128 us  [shards(): pl.pallas_call(cgls, out_shape=(jax.ShapeDtypeStruct((CROWS, COLS), F32),...]
    all_gather x4 -> x0, blocking collectives: 114 us -> none  [the longest x2 79.2 us: gradient_of(): lax.all_gather(residual.astype(jnp.bfloat16), 'cell', axis=0, tiled=True)]
    another operation x4 -> x0, loops' own time: 18.5 us -> none  [the longest x2 9.25 us: shards(): lax.fori_loop(0, used, forward_add_block, jnp.zeros((tile_rows, columns),...]
  transfers between devices with their start and end apart: 4 -> 0, of which waited for: 4 -> 0; matrix products, arithmetic and copies ran while one was open for 0% -> 0% of each run, Pallas kernels for 0% -> 0%
where the time goes in v1:
time: 133 us
  Pallas kernels  128 us (96%)
  local copies, waits for them, and re-layouts  3.85 us (3%)
    pallas_call x1, Pallas kernels, shards(): pl.pallas_call(cgls, out_shape=(jax.ShapeDtypeStruct((CROWS, COLS), F32),...  128 us
    unnamed x10, local copies, waits for them, and re-layouts  3.85 us

profile of v1, /device:TPU:1, one launch (start us, length us, event | category | flops | bytes accessed | tf_op | source)
XLA Modules:
  0.0 133.1 jit_solution(3812384862355048363)
XLA Ops:
  1.3 0.0 copy-start.2
  1.3 0.0 copy-start.3
  1.3 0.6 copy-done.2
  1.9 0.0 copy-done.3
  1.9 0.0 copy-start
  2.0 1.2 copy-done
  3.2 0.0 copy-start.1
  3.2 0.7 copy-done.1
  3.9 127.9 %cgls.1 = (f32[96,128]{1,0:T(8,128)S(1)}, f32[48,128]{1,0:T(8,128)S(1)}) custom-call(bf16[8,256,256]{2,1,0:T(8,128)(2,1)S(1)} %bitcast.1, s32[1,1,8]{2,1,0:T(1,128)S(1)} %copy-done.2, s32[1,1,8]{2,1,0:T(1,128)S(1)} %copy-done.3, s32[1,1]{1,0:T(1,128)S(6)} %copy.9.counts, f32[48,128]{1,0:T(8,128)S(1)} %copy-done.1), custom_call_target="tpu_custom_call" | custom-call | tf_op jit(solution)/shard_map/cgls/pallas_call | solution.py:311
  131.9 0.6 copy.10
  132.5 0.6 copy.11
Async XLA Ops:
  1.3 0.7 copy-start.2
  1.3 0.7 copy-start.3
  1.9 1.2 copy-start
  3.2 0.7 copy-start.1

commit v2 on v1

v2 whole, which is shorter than its diff:
```python
import jax
import jax.numpy as jnp
from jax import lax
from jax.experimental import pallas as pl
from jax.experimental.pallas import tpu as pltpu
from jax.sharding import PartitionSpec as P

F32 = jnp.float32
BF16 = jnp.bfloat16
MESH = pl.DeviceIdType.MESH
SLOTS = 8
BLOCK = 256
NY = 8
NZ = 8
NX = 4
N_DP = NY * 2
N_CELL = NZ * NX
TILE = 6 * BLOCK
DROWS = TILE // N_CELL
CROWS = TILE // N_DP
COLS = 128


def far_first(i, n):
    return n // 2 - (i + 1) // 2 if i % 2 == 1 else (n // 2 + i // 2) % n


def rows_at(ref, index, size):
    return ref.at[pl.ds(pl.multiple_of(index * size, size), size)]


def cgls(
    tiles_hbm,
    row_of,
    col_of,
    counts,
    observed,
    model_out,
    residual_out,
    tiles,
    tiles_t,
    pieces,
    prod,
    residual_full,
    direction_full,
    grad_send,
    pair_recv,
    grad_pair,
    grad_recv,
    image_send,
    image_recv,
    sums_mine,
    sums_dp,
    sums_mid,
    sums_cell,
    load_sem,
    gather_send_sem,
    gather_recv_sem,
    dir_send_sem,
    dir_recv_sem,
    fwd_send_sem,
    fwd_recv_sem,
    pair_send_sem,
    pair_recv_sem,
    grad_send_sem,
    grad_recv_sem,
    image_send_sem,
    image_recv_sem,
    small_send_sem,
    small_recv_sem,
):
    dp = lax.axis_index("dp")
    cell = lax.axis_index("cell")
    y, core = dp // 2, dp % 2
    z, x = cell // NX, cell % NX
    sibling = (y * 2 + 1 - core, cell)
    my_cells = pl.ds(pl.multiple_of(dp * CROWS, CROWS), CROWS)
    my_rows = pl.ds(pl.multiple_of(cell * DROWS, DROWS), DROWS)

    load = pltpu.make_async_copy(tiles_hbm, tiles, load_sem)
    load.start()

    def z_at(i):
        return (z + far_first(i, NZ)) % NZ

    def y_at(i):
        return (y + far_first(i, NY)) % NY

    def over_cells(step):
        for i in range(N_CELL - 1):
            step(z_at(i // NX) * NX + (x + far_first(i % NX, NX)) % NX, i // NX)

    def over_dp(step):
        for i in range(N_DP - 1):
            step(y_at(i // 2) * 2 + (core + 1 + i) % 2)

    def remote(src, dst, send, recv, device):
        return pltpu.make_async_remote_copy(
            src_ref=src, dst_ref=dst, send_sem=send, recv_sem=recv, device_id=device, device_id_type=MESH
        )

    def wait_bytes(ref, sem):
        pltpu.make_async_copy(ref, ref, sem).wait()

    barrier = pltpu.get_barrier_semaphore()
    over_cells(lambda p, _: pl.semaphore_signal(barrier, inc=1, device_id=(dp, p), device_id_type=MESH))
    over_dp(lambda p: pl.semaphore_signal(barrier, inc=1, device_id=(p, cell), device_id_type=MESH))
    residual_full[0, my_rows, :] = observed[...].astype(BF16)
    load.wait()
    for slot in range(SLOTS):
        tiles_t[slot] = tiles[slot].T
    pl.semaphore_wait(barrier, N_CELL + N_DP - 2)

    used = counts[0, 0]

    def apply(matrix, source, target, vector, send):
        for at in range(6):
            pieces[at] = vector[pl.ds(at * BLOCK, BLOCK), :]
        for slot in range(SLOTS):
            prod[slot] = jnp.dot(matrix[slot], pieces[source[0, 0, slot]], preferred_element_type=F32)

        def place(at, carry):
            total = jnp.zeros((BLOCK, COLS), F32)
            for slot in range(SLOTS):
                here = jnp.logical_and(target[0, 0, slot] == at, slot < used)
                total = total + here.astype(F32) * prod[slot]
            send[pl.ds(pl.multiple_of(at * BLOCK, BLOCK), BLOCK), :] = total.astype(send.dtype)
            return carry

        lax.fori_loop(0, 6, place, 0)

    def gather_cells(k):
        mine = residual_full.at[k, my_rows]
        over_cells(lambda p, _: remote(mine, mine, gather_send_sem.at[k], gather_recv_sem.at[k], (dp, p)).start())
        others = residual_full.at[k, pl.ds(0, (N_CELL - 1) * DROWS)]
        wait_bytes(others, gather_recv_sem.at[k])
        wait_bytes(others, gather_send_sem.at[k])

    def gather_dp(k):
        full = direction_full.at[k]
        mine = full.at[my_cells]
        for i in range(NY - 1):
            remote(mine, mine, dir_send_sem.at[k], dir_recv_sem.at[k, y], (y_at(i) * 2 + core, cell)).start()
        remote(mine, mine, fwd_send_sem.at[k], fwd_recv_sem.at[k], sibling).start()
        for i in range(NY - 1):
            src = y_at(NY - 2 - i)
            slot = rows_at(full, src * 2 + core, CROWS)
            wait_bytes(slot, dir_recv_sem.at[k, src])
            remote(slot, slot, fwd_send_sem.at[k], fwd_recv_sem.at[k], sibling).start()
        wait_bytes(full.at[pl.ds(0, NY * CROWS)], fwd_recv_sem.at[k])
        wait_bytes(full.at[pl.ds(0, NY * CROWS)], fwd_send_sem.at[k])
        wait_bytes(full.at[pl.ds(0, (NY - 1) * CROWS)], dir_send_sem.at[k])

    def scatter_dp(k):
        for i in range(NY):
            at = y_at(i)
            src = rows_at(grad_send.at[k], at * 2 + 1 - core, CROWS)
            remote(src, rows_at(pair_recv.at[k], at, CROWS), pair_send_sem.at[k], pair_recv_sem.at[k, at], sibling).start()
        slot = rows_at(grad_recv.at[k], y, CROWS)
        for i in range(NY):
            at = y_at(i)
            rows = pl.ds(pl.multiple_of(at * CROWS, CROWS), CROWS)
            wait_bytes(pair_recv.at[k, rows], pair_recv_sem.at[k, at])
            both = grad_send[k, pl.ds(pl.multiple_of((at * 2 + core) * CROWS, CROWS), CROWS), :] + pair_recv[k, rows, :]
            if i < NY - 1:
                grad_pair[k, rows, :] = both.astype(BF16)
                remote(
                    grad_pair.at[k, rows], slot, grad_send_sem.at[k], grad_recv_sem.at[k, y], (at * 2 + core, cell)
                ).start()
            else:
                total = both
        for i in range(NY - 1):
            src = y_at(NY - 2 - i)
            rows = pl.ds(pl.multiple_of(src * CROWS, CROWS), CROWS)
            wait_bytes(grad_recv.at[k, rows], grad_recv_sem.at[k, src])
            total = total + grad_recv[k, rows, :].astype(F32)
        wait_bytes(grad_recv.at[k, pl.ds(0, (NY - 1) * CROWS)], grad_send_sem.at[k])
        wait_bytes(pair_recv.at[k], pair_send_sem.at[k])
        return total

    def scatter_cells(k):
        slot = image_recv.at[k, my_rows]

        def send(p, group):
            remote(
                rows_at(image_send.at[k], p, DROWS), slot, image_send_sem.at[k], image_recv_sem.at[k, z], (dp, p)
            ).start()

        over_cells(send)
        image_recv[k, my_rows, :] = image_send[k, my_rows, :]
        total = jnp.zeros((DROWS, COLS), F32)
        for i in range(NZ):
            src = z_at(NZ - 1 - i)
            start = pl.multiple_of(src * NX * DROWS, NX * DROWS)
            count = NX - 1 if i == 0 else NX
            wait_bytes(image_recv.at[k, pl.ds(start, count * DROWS)], image_recv_sem.at[k, src])
            for j in range(NX):
                total = total + image_recv[k, pl.ds(start + j * DROWS, DROWS), :].astype(F32)
        wait_bytes(image_recv.at[k, pl.ds(0, (N_CELL - 1) * DROWS)], image_send_sem.at[k])
        return total

    def column(values):
        return jnp.sum(values, axis=0, keepdims=True)

    def sum_all(k, rows):
        sums_mine[k] = jnp.zeros((8, COLS), F32)
        for i, row in enumerate(rows):
            sums_mine[k, pl.ds(i, 1), :] = row
        mine = sums_mine.at[k]
        over_dp(
            lambda p: remote(mine, sums_dp.at[k, dp], small_send_sem.at[k, 0], small_recv_sem.at[k, 0], (p, cell)).start()
        )
        sums_dp[k, dp] = sums_mine[k]
        wait_bytes(sums_dp.at[k, pl.ds(0, N_DP - 1)], small_recv_sem.at[k, 0])
        sums_mid[k] = jnp.sum(sums_dp[k], axis=0)
        half = sums_mid.at[k]
        over_cells(
            lambda p, _: remote(
                half, sums_cell.at[k, cell], small_send_sem.at[k, 1], small_recv_sem.at[k, 1], (dp, p)
            ).start()
        )
        sums_cell[k, cell] = sums_mid[k]
        wait_bytes(sums_cell.at[k, pl.ds(0, N_CELL - 1)], small_recv_sem.at[k, 1])
        total = jnp.sum(sums_cell[k], axis=0)
        wait_bytes(sums_dp.at[k, pl.ds(0, N_DP - 1)], small_send_sem.at[k, 0])
        wait_bytes(sums_cell.at[k, pl.ds(0, N_CELL - 1)], small_send_sem.at[k, 1])
        return [total[i : i + 1] for i in range(len(rows))]

    gather_cells(0)
    apply(tiles_t, row_of, col_of, residual_full.at[0], grad_send.at[0])
    gradient = scatter_dp(0)
    model_out[...] = gradient

    direction_full[0, my_cells, :] = gradient.astype(BF16)
    gather_dp(0)
    apply(tiles, col_of, row_of, direction_full.at[0], image_send.at[0])
    image = scatter_cells(0)

    first = model_out[...]
    gamma, delta = sum_all(0, [column(first * first), column(image * image)])
    alpha = gamma / delta
    residual = observed[...] - alpha * image
    residual_out[...] = image

    residual_full[1, my_rows, :] = residual.astype(BF16)
    gather_cells(1)
    apply(tiles_t, row_of, col_of, residual_full.at[1], grad_send.at[1])
    gradient = scatter_dp(1)

    direction_full[1, my_cells, :] = gradient.astype(BF16)
    gather_dp(1)
    apply(tiles, col_of, row_of, direction_full.at[1], image_send.at[1])
    update = scatter_cells(1)
    image = residual_out[...]
    gamma_one, update_square, cross = sum_all(
        1, [column(gradient * gradient), column(update * update), column(update * image)]
    )
    beta = gamma_one / gamma
    delta_one = update_square + beta * (2.0 * cross + beta * delta)
    alpha_one = gamma_one / delta_one
    first = model_out[...]
    model_out[...] = alpha * first + alpha_one * (gradient + beta * first)
    residual_out[...] = observed[...] - alpha * image - alpha_one * (update + beta * image)


def shards(blocks, row_block, col_block, counts, observed):
    vmem = pl.BlockSpec(memory_space=pltpu.VMEM)
    smem = pl.BlockSpec(memory_space=pltpu.SMEM)
    dma = pltpu.SemaphoreType.DMA
    return pl.pallas_call(
        cgls,
        out_shape=(
            jax.ShapeDtypeStruct((CROWS, COLS), F32),
            jax.ShapeDtypeStruct((DROWS, COLS), F32),
        ),
        in_specs=[pl.BlockSpec(memory_space=pl.ANY), smem, smem, smem, vmem],
        out_specs=(vmem, vmem),
        scratch_shapes=[
            pltpu.VMEM((SLOTS, BLOCK, BLOCK), BF16),
            pltpu.VMEM((SLOTS, BLOCK, BLOCK), BF16),
            pltpu.VMEM((6, BLOCK, COLS), BF16),
            pltpu.VMEM((SLOTS, BLOCK, COLS), F32),
            pltpu.VMEM((2, TILE, COLS), BF16),
            pltpu.VMEM((2, TILE, COLS), BF16),
            pltpu.VMEM((2, TILE, COLS), F32),
            pltpu.VMEM((2, TILE // 2, COLS), F32),
            pltpu.VMEM((2, TILE // 2, COLS), BF16),
            pltpu.VMEM((2, TILE // 2, COLS), BF16),
            pltpu.VMEM((2, TILE, COLS), BF16),
            pltpu.VMEM((2, TILE, COLS), BF16),
            pltpu.VMEM((2, 8, COLS), F32),
            pltpu.VMEM((2, N_DP, 8, COLS), F32),
            pltpu.VMEM((2, 8, COLS), F32),
            pltpu.VMEM((2, N_CELL, 8, COLS), F32),
            dma,
            dma((2,)),
            dma((2,)),
            dma((2,)),
            dma((2, NY)),
            dma((2,)),
            dma((2,)),
            dma((2,)),
            dma((2, NY)),
            dma((2,)),
            dma((2, NY)),
            dma((2,)),
            dma((2, NZ)),
            dma((2, 2)),
            dma((2, 2)),
        ],
        compiler_params=pltpu.CompilerParams(
            collective_id=0, has_side_effects=True, vmem_limit_bytes=40 * 1024 * 1024
        ),
        name="cgls",
    )(blocks[0, 0], row_block, col_block, counts, observed)


def solution(mesh):
    in_specs = (
        P("dp", "cell", None, None, None),
        P("dp", "cell", None),
        P("dp", "cell", None),
        P("dp", "cell"),
        P(("dp", "cell"), None),
    )
    out_specs = (P(("cell", "dp"), None), P(("dp", "cell"), None))
    return jax.shard_map(shards, mesh=mesh, in_specs=in_specs, out_specs=out_specs, check_vma=False)
```

time: 133 us -> 125 us (0.940)
  Pallas kernels: 128 us -> 119 us
    pallas_call x1, Pallas kernels: 128 us -> 119 us  [shards(): pl.pallas_call(cgls, out_shape=(jax.ShapeDtypeStruct((CROWS, COLS), F32),...]
where the time goes in v2:
time: 125 us; the launch traced here: 124 us
  Pallas kernels  119 us (95%)
  local copies, waits for them, and re-layouts  3.85 us (3%)
  between operations  1.3 us (1%)
    pallas_call x1, Pallas kernels, shards(): pl.pallas_call(cgls, out_shape=(jax.ShapeDtypeStruct((CROWS, COLS), F32),...  119 us
    unnamed x10, local copies, waits for them, and re-layouts  3.85 us

profile of v2, /device:TPU:1, one launch (start us, length us, event | category | flops | bytes accessed | tf_op | source)
XLA Modules:
  0.0 124.5 jit_solution(17142574378871255355)
XLA Ops:
  1.3 0.0 copy-start.2
  1.3 0.0 copy-start.3
  1.3 0.6 copy-done.2
  1.9 0.0 copy-done.3
  1.9 0.0 copy-start
  2.0 1.2 copy-done
  3.2 0.0 copy-start.1
  3.2 0.7 copy-done.1
  3.9 119.3 %cgls.1 = (f32[96,128]{1,0:T(8,128)S(1)}, f32[48,128]{1,0:T(8,128)S(1)}) custom-call(bf16[8,256,256]{2,1,0:T(8,128)(2,1)S(1)} %bitcast.1, s32[1,1,8]{2,1,0:T(1,128)S(1)} %copy-done.2, s32[1,1,8]{2,1,0:T(1,128)S(1)} %copy-done.3, s32[1,1]{1,0:T(1,128)S(6)} %copy.9.counts, f32[48,128]{1,0:T(8,128)S(1)} %copy-done.1), custom_call_target="tpu_custom_call" | custom-call | tf_op jit(solution)/shard_map/cgls/pallas_call | solution.py:270
  123.2 0.6 copy.10
  123.8 0.6 copy.11
Async XLA Ops:
  1.3 0.7 copy-start.2
  1.3 0.7 copy-start.3
  1.9 1.2 copy-start
  3.2 0.7 copy-start.1

commit v3 on v2

--- a/solution.py
+++ b/solution.py
@@ -25,8 +25,12 @@
     return n // 2 - (i + 1) // 2 if i % 2 == 1 else (n // 2 + i // 2) % n
 
 
+def rows_of(index, size):
+    return pl.ds(pl.multiple_of(index * size, size), size)
+
+
 def rows_at(ref, index, size):
-    return ref.at[pl.ds(pl.multiple_of(index * size, size), size)]
+    return ref.at[rows_of(index, size)]
 
 
 def cgls(
@@ -48,6 +52,8 @@
     grad_pair,
     grad_recv,
     image_send,
+    line_recv,
+    image_line,
     image_recv,
     sums_mine,
     sums_dp,
@@ -55,7 +61,8 @@
     sums_cell,
     load_sem,
     gather_send_sem,
-    gather_recv_sem,
+    gather_z_sem,
+    gather_x_sem,
     dir_send_sem,
     dir_recv_sem,
     fwd_send_sem,
@@ -64,6 +71,8 @@
     pair_recv_sem,
     grad_send_sem,
     grad_recv_sem,
+    line_send_sem,
+    line_recv_sem,
     image_send_sem,
     image_recv_sem,
     small_send_sem,
@@ -83,12 +92,15 @@
     def z_at(i):
         return (z + far_first(i, NZ)) % NZ
 
+    def x_at(i):
+        return (x + far_first(i, NX)) % NX
+
     def y_at(i):
         return (y + far_first(i, NY)) % NY
 
     def over_cells(step):
         for i in range(N_CELL - 1):
-            step(z_at(i // NX) * NX + (x + far_first(i % NX, NX)) % NX, i // NX)
+            step(z_at(i // NX) * NX + x_at(i % NX))
 
     def over_dp(step):
         for i in range(N_DP - 1):
@@ -103,13 +115,15 @@
         pltpu.make_async_copy(ref, ref, sem).wait()
 
     barrier = pltpu.get_barrier_semaphore()
-    over_cells(lambda p, _: pl.semaphore_signal(barrier, inc=1, device_id=(dp, p), device_id_type=MESH))
-    over_dp(lambda p: pl.semaphore_signal(barrier, inc=1, device_id=(p, cell), device_id_type=MESH))
+    greet = [(dp, z_at(i) * NX + x) for i in range(NZ - 1)] + [(y_at(i) * 2 + core, cell) for i in range(NY - 1)]
+    greet += [(dp, z * NX + x_at(i)) for i in range(NX - 1)] + [sibling]
+    for device in greet:
+        pl.semaphore_signal(barrier, inc=1, device_id=device, device_id_type=MESH)
     residual_full[0, my_rows, :] = observed[...].astype(BF16)
     load.wait()
     for slot in range(SLOTS):
         tiles_t[slot] = tiles[slot].T
-    pl.semaphore_wait(barrier, N_CELL + N_DP - 2)
+    pl.semaphore_wait(barrier, len(greet))
 
     used = counts[0, 0]
 
@@ -130,11 +144,20 @@
         lax.fori_loop(0, 6, place, 0)
 
     def gather_cells(k):
-        mine = residual_full.at[k, my_rows]
-        over_cells(lambda p, _: remote(mine, mine, gather_send_sem.at[k], gather_recv_sem.at[k], (dp, p)).start())
-        others = residual_full.at[k, pl.ds(0, (N_CELL - 1) * DROWS)]
-        wait_bytes(others, gather_recv_sem.at[k])
-        wait_bytes(others, gather_send_sem.at[k])
+        full = residual_full.at[k]
+        mine = full.at[my_rows]
+        for i in range(NZ - 1):
+            remote(mine, mine, gather_send_sem.at[k], gather_z_sem.at[k, z], (dp, z_at(i) * NX + x)).start()
+        for i in range(NX - 1):
+            remote(mine, mine, gather_send_sem.at[k], gather_x_sem.at[k], (dp, z * NX + x_at(i))).start()
+        for i in range(NZ - 1):
+            src = z_at(NZ - 2 - i)
+            slot = rows_at(full, src * NX + x, DROWS)
+            wait_bytes(slot, gather_z_sem.at[k, src])
+            for j in range(NX - 1):
+                remote(slot, slot, gather_send_sem.at[k], gather_x_sem.at[k], (dp, z * NX + x_at(j))).start()
+        wait_bytes(full.at[pl.ds(0, NZ * (NX - 1) * DROWS)], gather_x_sem.at[k])
+        wait_bytes(full.at[pl.ds(0, (N_CELL - 1) * DROWS)], gather_send_sem.at[k])
 
     def gather_dp(k):
         full = direction_full.at[k]
@@ -179,24 +202,33 @@
         return total
 
     def scatter_cells(k):
-        slot = image_recv.at[k, my_rows]
-
-        def send(p, group):
-            remote(
-                rows_at(image_send.at[k], p, DROWS), slot, image_send_sem.at[k], image_recv_sem.at[k, z], (dp, p)
-            ).start()
-
-        over_cells(send)
-        image_recv[k, my_rows, :] = image_send[k, my_rows, :]
-        total = jnp.zeros((DROWS, COLS), F32)
         for i in range(NZ):
-            src = z_at(NZ - 1 - i)
-            start = pl.multiple_of(src * NX * DROWS, NX * DROWS)
-            count = NX - 1 if i == 0 else NX
-            wait_bytes(image_recv.at[k, pl.ds(start, count * DROWS)], image_recv_sem.at[k, src])
-            for j in range(NX):
-                total = total + image_recv[k, pl.ds(start + j * DROWS, DROWS), :].astype(F32)
-        wait_bytes(image_recv.at[k, pl.ds(0, (N_CELL - 1) * DROWS)], image_send_sem.at[k])
+            to = z_at(i)
+            slot = rows_at(line_recv.at[k], to * NX + x, DROWS)
+            for j in range(NX - 1):
+                src = rows_at(image_send.at[k], to * NX + x_at(j), DROWS)
+                remote(src, slot, line_send_sem.at[k], line_recv_sem.at[k, to], (dp, z * NX + x_at(j))).start()
+        for i in range(NZ):
+            to = z_at(i)
+            wait_bytes(line_recv.at[k, pl.ds(0, (NX - 1) * DROWS)], line_recv_sem.at[k, to])
+            total = image_send[k, rows_of(to * NX + x, DROWS), :].astype(F32)
+            for j in range(NX - 1):
+                total = total + line_recv[k, rows_of(to * NX + x_at(j), DROWS), :].astype(F32)
+            if i < NZ - 1:
+                image_line[k, rows_of(to, DROWS), :] = total
+                remote(
+                    rows_at(image_line.at[k], to, DROWS),
+                    rows_at(image_recv.at[k], z, DROWS),
+                    image_send_sem.at[k],
+                    image_recv_sem.at[k, z],
+                    (dp, to * NX + x),
+                ).start()
+        for i in range(NZ - 1):
+            src = z_at(NZ - 2 - i)
+            wait_bytes(rows_at(image_recv.at[k], src, DROWS), image_recv_sem.at[k, src])
+            total = total + image_recv[k, rows_of(src, DROWS), :]
+        wait_bytes(line_recv.at[k, pl.ds(0, NZ * (NX - 1) * DROWS)], line_send_sem.at[k])
+        wait_bytes(image_recv.at[k, pl.ds(0, (NZ - 1) * DROWS)], image_send_sem.at[k])
         return total
 
     def column(values):
@@ -215,7 +247,7 @@
         sums_mid[k] = jnp.sum(sums_dp[k], axis=0)
         half = sums_mid.at[k]
         over_cells(
-            lambda p, _: remote(
+            lambda p: remote(
                 half, sums_cell.at[k, cell], small_send_sem.at[k, 1], small_recv_sem.at[k, 1], (dp, p)
             ).start()
         )
@@ -288,12 +320,15 @@
             pltpu.VMEM((2, TILE // 2, COLS), BF16),
             pltpu.VMEM((2, TILE, COLS), BF16),
             pltpu.VMEM((2, TILE, COLS), BF16),
+            pltpu.VMEM((2, NZ * DROWS, COLS), F32),
+            pltpu.VMEM((2, NZ * DROWS, COLS), F32),
             pltpu.VMEM((2, 8, COLS), F32),
             pltpu.VMEM((2, N_DP, 8, COLS), F32),
             pltpu.VMEM((2, 8, COLS), F32),
             pltpu.VMEM((2, N_CELL, 8, COLS), F32),
             dma,
             dma((2,)),
+            dma((2, NZ)),
             dma((2,)),
             dma((2,)),
             dma((2, NY)),
@@ -303,13 +338,15 @@
             dma((2, NY)),
             dma((2,)),
             dma((2, NY)),
+            dma((2,)),
+            dma((2, NZ)),
             dma((2,)),
             dma((2, NZ)),
             dma((2, 2)),
             dma((2, 2)),
         ],
         compiler_params=pltpu.CompilerParams(
-            collective_id=0, has_side_effects=True, vmem_limit_bytes=40 * 1024 * 1024
+            collective_id=0, has_side_effects=True, vmem_limit_bytes=60 * 1024 * 1024
         ),
         name="cgls",
     )(blocks[0, 0], row_block, col_block, counts, observed)

time: 125 us -> 116 us (0.928)
  Pallas kernels: 119 us -> 112 us
  local copies, waits for them, and re-layouts: 3.85 us -> 2.04 us
    pallas_call x1, Pallas kernels: 119 us -> 112 us  [shards(): pl.pallas_call(cgls, out_shape=(jax.ShapeDtypeStruct((CROWS, COLS), F32),...]
    unnamed x10 -> x4, local copies, waits for them, and re-layouts: 3.85 us -> 2.04 us
where the time goes in v3:
time: 116 us; the launch traced here: 115 us
  Pallas kernels  112 us (97%)
  local copies, waits for them, and re-layouts  2.04 us (2%)
  between operations  1.29 us (1%)
    pallas_call x1, Pallas kernels, shards(): pl.pallas_call(cgls, out_shape=(jax.ShapeDtypeStruct((CROWS, COLS), F32),...  112 us

profile of v3, /device:TPU:1, one launch (start us, length us, event | category | flops | bytes accessed | tf_op | source)
XLA Modules:
  0.0 115.5 jit_solution(10756279604321160245)
XLA Ops:
  1.3 112.2 %cgls.1 = (f32[96,128]{1,0:T(8,128)}, f32[48,128]{1,0:T(8,128)}) custom-call(bf16[8,256,256]{2,1,0:T(8,128)(2,1)} %bitcast.1, s32[1,1,8]{2,1,0:T(1,128)} %row_of.1, s32[1,1,8]{2,1,0:T(1,128)} %col_of.1, s32[1,1]{1,0:T(1,128)S(6)} %copy.9.counts, f32[48,128]{1,0:T(8,128)} %observed.1), custom_call_target="tpu_custom_call" | custom-call | tf_op jit(solution)/shard_map/cgls/pallas_call | solution.py:302
  113.5 0.0 copy-start
  113.5 1.4 %copy.10 = f32[96,128]{1,0:T(8,128)} copy(f32[96,128]{1,0:T(8,128)} %get-tuple-element.4) | data formatting | bytes 98304
  114.9 0.0 copy-done
  114.9 0.6 copy.11
Async XLA Ops:
  113.5 1.4 %copy-start = (f32[48,128]{1,0:T(8,128)S(1)}, f32[48,128]{1,0:T(8,128)}, u32[]{:S(2)}) copy-start(f32[48,128]{1,0:T(8,128)} %get-tuple-element.5) | copy-start | bytes 73732

commit v4 on v3

--- a/solution.py
+++ b/solution.py
@@ -19,6 +19,7 @@
 DROWS = TILE // N_CELL
 CROWS = TILE // N_DP
 COLS = 128
+TINY = 1e-30
 
 
 def far_first(i, n):
@@ -44,7 +45,9 @@
     tiles,
     tiles_t,
     pieces,
+    wide_pieces,
     prod,
+    image_exact,
     residual_full,
     direction_full,
     grad_send,
@@ -127,23 +130,29 @@
 
     used = counts[0, 0]
 
-    def apply(matrix, source, target, vector, send):
+    def multiply(matrix, source):
+        for slot in range(SLOTS):
+            prod[slot] = jnp.dot(matrix[slot], pieces[source[0, 0, slot]], preferred_element_type=F32)
+
+    def apply(matrix, source, target, vector, sends):
         for at in range(6):
             pieces[at] = vector[pl.ds(at * BLOCK, BLOCK), :]
-        for slot in range(SLOTS):
-            prod[slot] = jnp.dot(matrix[slot], pieces[source[0, 0, slot]], preferred_element_type=F32)
-
-        def place(at, carry):
+        multiply(matrix, source)
+        place(target, sends)
+
+    def place(target, sends):
+        def one(at, carry):
             total = jnp.zeros((BLOCK, COLS), F32)
             for slot in range(SLOTS):
                 here = jnp.logical_and(target[0, 0, slot] == at, slot < used)
                 total = total + here.astype(F32) * prod[slot]
-            send[pl.ds(pl.multiple_of(at * BLOCK, BLOCK), BLOCK), :] = total.astype(send.dtype)
+            for send in sends:
+                send[rows_of(at, BLOCK), :] = total.astype(send.dtype)
             return carry
 
-        lax.fori_loop(0, 6, place, 0)
-
-    def gather_cells(k):
+        lax.fori_loop(0, 6, one, 0)
+
+    def gather_cells(k, between=None):
         full = residual_full.at[k]
         mine = full.at[my_rows]
         for i in range(NZ - 1):
@@ -151,6 +160,8 @@
         for i in range(NX - 1):
             remote(mine, mine, gather_send_sem.at[k], gather_x_sem.at[k], (dp, z * NX + x_at(i))).start()
         for i in range(NZ - 1):
+            if i == 4 and between is not None:
+                between()
             src = z_at(NZ - 2 - i)
             slot = rows_at(full, src * NX + x, DROWS)
             wait_bytes(slot, gather_z_sem.at[k, src])
@@ -211,7 +222,7 @@
         for i in range(NZ):
             to = z_at(i)
             wait_bytes(line_recv.at[k, pl.ds(0, (NX - 1) * DROWS)], line_recv_sem.at[k, to])
-            total = image_send[k, rows_of(to * NX + x, DROWS), :].astype(F32)
+            total = image_exact[rows_of(to * NX + x, DROWS), :]
             for j in range(NX - 1):
                 total = total + line_recv[k, rows_of(to * NX + x_at(j), DROWS), :].astype(F32)
             if i < NZ - 1:
@@ -234,7 +245,12 @@
     def column(values):
         return jnp.sum(values, axis=0, keepdims=True)
 
-    def sum_all(k, rows):
+    def size_of(values):
+        most = jnp.max(jnp.abs(values), axis=0, keepdims=True)
+        unit = values * (1.0 / jnp.maximum(most, TINY))
+        return most * jnp.sqrt(column(unit * unit))
+
+    def sum_start(k, rows):
         sums_mine[k] = jnp.zeros((8, COLS), F32)
         for i, row in enumerate(rows):
             sums_mine[k, pl.ds(i, 1), :] = row
@@ -243,8 +259,12 @@
             lambda p: remote(mine, sums_dp.at[k, dp], small_send_sem.at[k, 0], small_recv_sem.at[k, 0], (p, cell)).start()
         )
         sums_dp[k, dp] = sums_mine[k]
+
+    def sum_middle(k, extra=None):
         wait_bytes(sums_dp.at[k, pl.ds(0, N_DP - 1)], small_recv_sem.at[k, 0])
         sums_mid[k] = jnp.sum(sums_dp[k], axis=0)
+        if extra is not None:
+            sums_mid[k, pl.ds(7, 1), :] = extra
         half = sums_mid.at[k]
         over_cells(
             lambda p: remote(
@@ -252,41 +272,61 @@
             ).start()
         )
         sums_cell[k, cell] = sums_mid[k]
+
+    def sum_end(k, n):
         wait_bytes(sums_cell.at[k, pl.ds(0, N_CELL - 1)], small_recv_sem.at[k, 1])
         total = jnp.sum(sums_cell[k], axis=0)
         wait_bytes(sums_dp.at[k, pl.ds(0, N_DP - 1)], small_send_sem.at[k, 0])
         wait_bytes(sums_cell.at[k, pl.ds(0, N_CELL - 1)], small_send_sem.at[k, 1])
-        return [total[i : i + 1] for i in range(len(rows))]
+        return [total[i : i + 1] for i in range(n)]
 
     gather_cells(0)
-    apply(tiles_t, row_of, col_of, residual_full.at[0], grad_send.at[0])
+    apply(tiles_t, row_of, col_of, residual_full.at[0], [grad_send.at[0]])
     gradient = scatter_dp(0)
     model_out[...] = gradient
 
     direction_full[0, my_cells, :] = gradient.astype(BF16)
     gather_dp(0)
-    apply(tiles, col_of, row_of, direction_full.at[0], image_send.at[0])
+    apply(tiles, col_of, row_of, direction_full.at[0], [image_send.at[0], image_exact])
     image = scatter_cells(0)
+    residual_out[...] = image
 
     first = model_out[...]
-    gamma, delta = sum_all(0, [column(first * first), column(image * image)])
+    sum_start(0, [column(first * first), column(image * image)])
+    observed_size = size_of(observed[...])
+    scale = jnp.clip(observed_size / jnp.maximum(size_of(image), TINY), 1e-18, 1e18)
+    scale = jnp.where(observed_size > 0.0, scale, 1.0)
+    residual_full[1, my_rows, :] = (observed[...] - scale * image).astype(BF16)
+    inverse = 1.0 / scale
+    gather_cells(1, lambda: sum_middle(0, inverse))
+    gamma, delta = sum_end(0, 2)
     alpha = gamma / delta
-    residual = observed[...] - alpha * image
-    residual_out[...] = image
-
-    residual_full[1, my_rows, :] = residual.astype(BF16)
-    gather_cells(1)
-    apply(tiles_t, row_of, col_of, residual_full.at[1], grad_send.at[1])
+
+    for c in range(N_CELL):
+        share = alpha * sums_cell[0, c, pl.ds(7, 1), :]
+        for part in range(DROWS // 16):
+            at = c * DROWS + part * 16
+            old = residual_full[0, pl.ds(at, 16), :].astype(F32)
+            new = residual_full[1, pl.ds(at, 16), :].astype(F32)
+            value = old + share * (new - old)
+            high = value.astype(BF16)
+            into = pl.ds(at % BLOCK, 16)
+            wide_pieces[at // BLOCK, into, pl.ds(0, COLS)] = high
+            wide_pieces[at // BLOCK, into, pl.ds(COLS, COLS)] = (value - high.astype(F32)).astype(BF16)
+    for slot in range(SLOTS):
+        both = jnp.dot(tiles_t[slot], wide_pieces[row_of[0, 0, slot]], preferred_element_type=F32)
+        prod[slot] = both[:, :COLS] + both[:, COLS:]
+    place(col_of, [grad_send.at[1]])
     gradient = scatter_dp(1)
 
     direction_full[1, my_cells, :] = gradient.astype(BF16)
     gather_dp(1)
-    apply(tiles, col_of, row_of, direction_full.at[1], image_send.at[1])
+    apply(tiles, col_of, row_of, direction_full.at[1], [image_send.at[1], image_exact])
     update = scatter_cells(1)
     image = residual_out[...]
-    gamma_one, update_square, cross = sum_all(
-        1, [column(gradient * gradient), column(update * update), column(update * image)]
-    )
+    sum_start(1, [column(gradient * gradient), column(update * update), column(update * image)])
+    sum_middle(1)
+    gamma_one, update_square, cross = sum_end(1, 3)
     beta = gamma_one / gamma
     delta_one = update_square + beta * (2.0 * cross + beta * delta)
     alpha_one = gamma_one / delta_one
@@ -311,7 +351,9 @@
             pltpu.VMEM((SLOTS, BLOCK, BLOCK), BF16),
             pltpu.VMEM((SLOTS, BLOCK, BLOCK), BF16),
             pltpu.VMEM((6, BLOCK, COLS), BF16),
+            pltpu.VMEM((6, BLOCK, 2 * COLS), BF16),
             pltpu.VMEM((SLOTS, BLOCK, COLS), F32),
+            pltpu.VMEM((TILE, COLS), F32),
             pltpu.VMEM((2, TILE, COLS), BF16),
             pltpu.VMEM((2, TILE, COLS), BF16),
             pltpu.VMEM((2, TILE, COLS), F32),

time: 116 us -> 109 us (0.940)
  Pallas kernels: 112 us -> 105 us
    pallas_call x1, Pallas kernels: 112 us -> 105 us  [shards(): pl.pallas_call(cgls, out_shape=(jax.ShapeDtypeStruct((CROWS, COLS), F32),...]
where the time goes in v4:
time: 109 us
  Pallas kernels  105 us (96%)
  local copies, waits for them, and re-layouts  2.04 us (2%)
  between operations  1.29 us (1%)
    pallas_call x1, Pallas kernels, shards(): pl.pallas_call(cgls, out_shape=(jax.ShapeDtypeStruct((CROWS, COLS), F32),...  105 us

profile of v4, /device:TPU:1, one launch (start us, length us, event | category | flops | bytes accessed | tf_op | source)
XLA Modules:
  0.0 108.6 jit_solution(15978360399570304018)
XLA Ops:
  1.3 105.2 %cgls.1 = (f32[96,128]{1,0:T(8,128)}, f32[48,128]{1,0:T(8,128)}) custom-call(bf16[8,256,256]{2,1,0:T(8,128)(2,1)} %bitcast.1, s32[1,1,8]{2,1,0:T(1,128)} %row_of.1, s32[1,1,8]{2,1,0:T(1,128)} %col_of.1, s32[1,1]{1,0:T(1,128)S(6)} %copy.9.counts, f32[48,128]{1,0:T(8,128)} %observed.1), custom_call_target="tpu_custom_call" | custom-call | tf_op jit(solution)/shard_map/cgls/pallas_call | solution.py:342
  106.5 0.0 copy-start
  106.5 1.4 %copy.10 = f32[96,128]{1,0:T(8,128)} copy(f32[96,128]{1,0:T(8,128)} %get-tuple-element.4) | data formatting | bytes 98304
  108.0 0.0 copy-done
  108.0 0.6 copy.11
Async XLA Ops:
  106.5 1.4 %copy-start = (f32[48,128]{1,0:T(8,128)S(1)}, f32[48,128]{1,0:T(8,128)}, u32[]{:S(2)}) copy-start(f32[48,128]{1,0:T(8,128)} %get-tuple-element.5) | copy-start | bytes 73732

commit v5 on v4

--- a/solution.py
+++ b/solution.py
@@ -18,6 +18,7 @@
 TILE = 6 * BLOCK
 DROWS = TILE // N_CELL
 CROWS = TILE // N_DP
+HALF = CROWS // 2
 COLS = 128
 TINY = 1e-30
 
@@ -48,6 +49,7 @@
     wide_pieces,
     prod,
     image_exact,
+    gradient,
     residual_full,
     direction_full,
     grad_send,
@@ -86,7 +88,6 @@
     y, core = dp // 2, dp % 2
     z, x = cell // NX, cell % NX
     sibling = (y * 2 + 1 - core, cell)
-    my_cells = pl.ds(pl.multiple_of(dp * CROWS, CROWS), CROWS)
     my_rows = pl.ds(pl.multiple_of(cell * DROWS, DROWS), DROWS)
 
     load = pltpu.make_async_copy(tiles_hbm, tiles, load_sem)
@@ -168,49 +169,54 @@
             for j in range(NX - 1):
                 remote(slot, slot, gather_send_sem.at[k], gather_x_sem.at[k], (dp, z * NX + x_at(j))).start()
         wait_bytes(full.at[pl.ds(0, NZ * (NX - 1) * DROWS)], gather_x_sem.at[k])
-        wait_bytes(full.at[pl.ds(0, (N_CELL - 1) * DROWS)], gather_send_sem.at[k])
-
-    def gather_dp(k):
+
+    def pass_dp(k):
         full = direction_full.at[k]
-        mine = full.at[my_cells]
-        for i in range(NY - 1):
-            remote(mine, mine, dir_send_sem.at[k], dir_recv_sem.at[k, y], (y_at(i) * 2 + core, cell)).start()
-        remote(mine, mine, fwd_send_sem.at[k], fwd_recv_sem.at[k], sibling).start()
-        for i in range(NY - 1):
-            src = y_at(NY - 2 - i)
-            slot = rows_at(full, src * 2 + core, CROWS)
-            wait_bytes(slot, dir_recv_sem.at[k, src])
-            remote(slot, slot, fwd_send_sem.at[k], fwd_recv_sem.at[k], sibling).start()
-        wait_bytes(full.at[pl.ds(0, NY * CROWS)], fwd_recv_sem.at[k])
-        wait_bytes(full.at[pl.ds(0, NY * CROWS)], fwd_send_sem.at[k])
-        wait_bytes(full.at[pl.ds(0, (NY - 1) * CROWS)], dir_send_sem.at[k])
-
-    def scatter_dp(k):
+
+        def half(index, h):
+            return pl.ds(pl.multiple_of(index * CROWS + h * HALF, HALF), HALF)
+
         for i in range(NY):
             at = y_at(i)
             src = rows_at(grad_send.at[k], at * 2 + 1 - core, CROWS)
             remote(src, rows_at(pair_recv.at[k], at, CROWS), pair_send_sem.at[k], pair_recv_sem.at[k, at], sibling).start()
-        slot = rows_at(grad_recv.at[k], y, CROWS)
-        for i in range(NY):
-            at = y_at(i)
-            rows = pl.ds(pl.multiple_of(at * CROWS, CROWS), CROWS)
-            wait_bytes(pair_recv.at[k, rows], pair_recv_sem.at[k, at])
-            both = grad_send[k, pl.ds(pl.multiple_of((at * 2 + core) * CROWS, CROWS), CROWS), :] + pair_recv[k, rows, :]
-            if i < NY - 1:
-                grad_pair[k, rows, :] = both.astype(BF16)
-                remote(
-                    grad_pair.at[k, rows], slot, grad_send_sem.at[k], grad_recv_sem.at[k, y], (at * 2 + core, cell)
-                ).start()
-            else:
-                total = both
-        for i in range(NY - 1):
-            src = y_at(NY - 2 - i)
-            rows = pl.ds(pl.multiple_of(src * CROWS, CROWS), CROWS)
-            wait_bytes(grad_recv.at[k, rows], grad_recv_sem.at[k, src])
-            total = total + grad_recv[k, rows, :].astype(F32)
-        wait_bytes(grad_recv.at[k, pl.ds(0, (NY - 1) * CROWS)], grad_send_sem.at[k])
-        wait_bytes(pair_recv.at[k], pair_send_sem.at[k])
-        return total
+        totals = []
+        for h in range(2):
+            for i in range(NY):
+                at = y_at(i)
+                if h == 0:
+                    wait_bytes(rows_at(pair_recv.at[k], at, CROWS), pair_recv_sem.at[k, at])
+                both = grad_send[k, half(at * 2 + core, h), :] + pair_recv[k, half(at, h), :]
+                if i < NY - 1:
+                    grad_pair[k, half(at, h), :] = both.astype(BF16)
+                    remote(
+                        grad_pair.at[k, half(at, h)],
+                        grad_recv.at[k, half(y, h)],
+                        grad_send_sem.at[k],
+                        grad_recv_sem.at[k, h, y],
+                        (at * 2 + core, cell),
+                    ).start()
+                else:
+                    totals.append(both)
+        for h in range(2):
+            total = totals[h]
+            for i in range(NY - 1):
+                src = y_at(NY - 2 - i)
+                wait_bytes(grad_recv.at[k, half(src, h)], grad_recv_sem.at[k, h, src])
+                total = total + grad_recv[k, half(src, h), :].astype(F32)
+            gradient[k, pl.ds(h * HALF, HALF), :] = total
+            mine = full.at[half(dp, h)]
+            direction_full[k, half(dp, h), :] = total.astype(BF16)
+            for i in range(NY - 1):
+                remote(mine, mine, dir_send_sem.at[k], dir_recv_sem.at[k, h, y], (y_at(i) * 2 + core, cell)).start()
+            remote(mine, mine, fwd_send_sem.at[k], fwd_recv_sem.at[k], sibling).start()
+        for h in range(2):
+            for i in range(NY - 1):
+                src = y_at(NY - 2 - i)
+                slot = full.at[half(src * 2 + core, h)]
+                wait_bytes(slot, dir_recv_sem.at[k, h, src])
+                remote(slot, slot, fwd_send_sem.at[k], fwd_recv_sem.at[k], sibling).start()
+        wait_bytes(full.at[pl.ds(0, NY * CROWS)], fwd_recv_sem.at[k])
 
     def scatter_cells(k):
         for i in range(NZ):
@@ -238,8 +244,6 @@
             src = z_at(NZ - 2 - i)
             wait_bytes(rows_at(image_recv.at[k], src, DROWS), image_recv_sem.at[k, src])
             total = total + image_recv[k, rows_of(src, DROWS), :]
-        wait_bytes(line_recv.at[k, pl.ds(0, NZ * (NX - 1) * DROWS)], line_send_sem.at[k])
-        wait_bytes(image_recv.at[k, pl.ds(0, (NZ - 1) * DROWS)], image_send_sem.at[k])
         return total
 
     def column(values):
@@ -276,22 +280,28 @@
     def sum_end(k, n):
         wait_bytes(sums_cell.at[k, pl.ds(0, N_CELL - 1)], small_recv_sem.at[k, 1])
         total = jnp.sum(sums_cell[k], axis=0)
+        return [total[i : i + 1] for i in range(n)]
+
+    def wait_sends(k):
+        wait_bytes(residual_full.at[k, pl.ds(0, (N_CELL - 1) * DROWS)], gather_send_sem.at[k])
+        wait_bytes(pair_recv.at[k], pair_send_sem.at[k])
+        wait_bytes(grad_recv.at[k, pl.ds(0, (NY - 1) * CROWS)], grad_send_sem.at[k])
+        wait_bytes(direction_full.at[k, pl.ds(0, (NY - 1) * CROWS)], dir_send_sem.at[k])
+        wait_bytes(direction_full.at[k, pl.ds(0, NY * CROWS)], fwd_send_sem.at[k])
+        wait_bytes(line_recv.at[k, pl.ds(0, NZ * (NX - 1) * DROWS)], line_send_sem.at[k])
+        wait_bytes(image_recv.at[k, pl.ds(0, (NZ - 1) * DROWS)], image_send_sem.at[k])
         wait_bytes(sums_dp.at[k, pl.ds(0, N_DP - 1)], small_send_sem.at[k, 0])
         wait_bytes(sums_cell.at[k, pl.ds(0, N_CELL - 1)], small_send_sem.at[k, 1])
-        return [total[i : i + 1] for i in range(n)]
 
     gather_cells(0)
     apply(tiles_t, row_of, col_of, residual_full.at[0], [grad_send.at[0]])
-    gradient = scatter_dp(0)
-    model_out[...] = gradient
-
-    direction_full[0, my_cells, :] = gradient.astype(BF16)
-    gather_dp(0)
+    pass_dp(0)
+
     apply(tiles, col_of, row_of, direction_full.at[0], [image_send.at[0], image_exact])
     image = scatter_cells(0)
     residual_out[...] = image
 
-    first = model_out[...]
+    first = gradient[0]
     sum_start(0, [column(first * first), column(image * image)])
     observed_size = size_of(observed[...])
     scale = jnp.clip(observed_size / jnp.maximum(size_of(image), TINY), 1e-18, 1e18)
@@ -317,22 +327,23 @@
         both = jnp.dot(tiles_t[slot], wide_pieces[row_of[0, 0, slot]], preferred_element_type=F32)
         prod[slot] = both[:, :COLS] + both[:, COLS:]
     place(col_of, [grad_send.at[1]])
-    gradient = scatter_dp(1)
-
-    direction_full[1, my_cells, :] = gradient.astype(BF16)
-    gather_dp(1)
+    pass_dp(1)
+
     apply(tiles, col_of, row_of, direction_full.at[1], [image_send.at[1], image_exact])
     update = scatter_cells(1)
     image = residual_out[...]
-    sum_start(1, [column(gradient * gradient), column(update * update), column(update * image)])
+    second = gradient[1]
+    sum_start(1, [column(second * second), column(update * update), column(update * image)])
     sum_middle(1)
     gamma_one, update_square, cross = sum_end(1, 3)
     beta = gamma_one / gamma
     delta_one = update_square + beta * (2.0 * cross + beta * delta)
     alpha_one = gamma_one / delta_one
-    first = model_out[...]
-    model_out[...] = alpha * first + alpha_one * (gradient + beta * first)
+    first = gradient[0]
+    model_out[...] = alpha * first + alpha_one * (gradient[1] + beta * first)
     residual_out[...] = observed[...] - alpha * image - alpha_one * (update + beta * image)
+    wait_sends(0)
+    wait_sends(1)
 
 
 def shards(blocks, row_block, col_block, counts, observed):
@@ -354,6 +365,7 @@
             pltpu.VMEM((6, BLOCK, 2 * COLS), BF16),
             pltpu.VMEM((SLOTS, BLOCK, COLS), F32),
             pltpu.VMEM((TILE, COLS), F32),
+            pltpu.VMEM((2, CROWS, COLS), F32),
             pltpu.VMEM((2, TILE, COLS), BF16),
             pltpu.VMEM((2, TILE, COLS), BF16),
             pltpu.VMEM((2, TILE, COLS), F32),
@@ -373,13 +385,13 @@
             dma((2, NZ)),
             dma((2,)),
             dma((2,)),
+            dma((2, 2, NY)),
+            dma((2,)),
+            dma((2,)),
+            dma((2,)),
             dma((2, NY)),
             dma((2,)),
-            dma((2,)),
-            dma((2,)),
-            dma((2, NY)),
-            dma((2,)),
-            dma((2, NY)),
+            dma((2, 2, NY)),
             dma((2,)),
             dma((2, NZ)),
             dma((2,)),

time: 109 us -> 105 us (0.963)
  Pallas kernels: 105 us -> 101 us
    pallas_call x1, Pallas kernels: 105 us -> 101 us  [shards(): pl.pallas_call(cgls, out_shape=(jax.ShapeDtypeStruct((CROWS, COLS), F32),...]
where the time goes in v5:
time: 105 us
  Pallas kernels  101 us (96%)
  local copies, waits for them, and re-layouts  2.04 us (2%)
  between operations  1.29 us (1%)
    pallas_call x1, Pallas kernels, shards(): pl.pallas_call(cgls, out_shape=(jax.ShapeDtypeStruct((CROWS, COLS), F32),...  101 us

profile of v5, /device:TPU:1, one launch (start us, length us, event | category | flops | bytes accessed | tf_op | source)
XLA Modules:
  0.0 104.7 jit_solution(16097784144107621442)
XLA Ops:
  1.3 101.3 %cgls.1 = (f32[96,128]{1,0:T(8,128)}, f32[48,128]{1,0:T(8,128)}) custom-call(bf16[8,256,256]{2,1,0:T(8,128)(2,1)} %bitcast.1, s32[1,1,8]{2,1,0:T(1,128)} %row_of.1, s32[1,1,8]{2,1,0:T(1,128)} %col_of.1, s32[1,1]{1,0:T(1,128)S(6)} %copy.9.counts, f32[48,128]{1,0:T(8,128)} %observed.1), custom_call_target="tpu_custom_call" | custom-call | tf_op jit(solution)/shard_map/cgls/pallas_call | solution.py:353
  102.6 0.0 copy-start
  102.6 1.4 %copy.10 = f32[96,128]{1,0:T(8,128)} copy(f32[96,128]{1,0:T(8,128)} %get-tuple-element.4) | data formatting | bytes 98304
  104.1 0.0 copy-done
  104.1 0.6 copy.11
Async XLA Ops:
  102.6 1.4 %copy-start = (f32[48,128]{1,0:T(8,128)S(1)}, f32[48,128]{1,0:T(8,128)}, u32[]{:S(2)}) copy-start(f32[48,128]{1,0:T(8,128)} %get-tuple-element.5) | copy-start | bytes 73732

commit v6 on v5

--- a/solution.py
+++ b/solution.py
@@ -64,7 +64,13 @@
     sums_dp,
     sums_mid,
     sums_cell,
+    pair_sum,
+    inverse_mine,
+    inverse,
+    scalars,
     load_sem,
+    scale_send_sem,
+    scale_recv_sem,
     gather_send_sem,
     gather_z_sem,
     gather_x_sem,
@@ -153,13 +159,15 @@
 
         lax.fori_loop(0, 6, one, 0)
 
-    def gather_cells(k, between=None):
+    def gather_cells(k, between=None, beside=None):
         full = residual_full.at[k]
         mine = full.at[my_rows]
         for i in range(NZ - 1):
             remote(mine, mine, gather_send_sem.at[k], gather_z_sem.at[k, z], (dp, z_at(i) * NX + x)).start()
         for i in range(NX - 1):
             remote(mine, mine, gather_send_sem.at[k], gather_x_sem.at[k], (dp, z * NX + x_at(i))).start()
+        if beside is not None:
+            beside()
         for i in range(NZ - 1):
             if i == 4 and between is not None:
                 between()
@@ -170,7 +178,7 @@
                 remote(slot, slot, gather_send_sem.at[k], gather_x_sem.at[k], (dp, z * NX + x_at(j))).start()
         wait_bytes(full.at[pl.ds(0, NZ * (NX - 1) * DROWS)], gather_x_sem.at[k])
 
-    def pass_dp(k):
+    def pass_dp(k, factor=None):
         full = direction_full.at[k]
 
         def half(index, h):
@@ -180,6 +188,8 @@
             at = y_at(i)
             src = rows_at(grad_send.at[k], at * 2 + 1 - core, CROWS)
             remote(src, rows_at(pair_recv.at[k], at, CROWS), pair_send_sem.at[k], pair_recv_sem.at[k, at], sibling).start()
+        if factor is not None:
+            share = factor()
         totals = []
         for h in range(2):
             for i in range(NY):
@@ -187,6 +197,10 @@
                 if h == 0:
                     wait_bytes(rows_at(pair_recv.at[k], at, CROWS), pair_recv_sem.at[k, at])
                 both = grad_send[k, half(at * 2 + core, h), :] + pair_recv[k, half(at, h), :]
+                if factor is None:
+                    pair_sum[half(at, h), :] = both
+                else:
+                    both = pair_sum[half(at, h), :] + share * both
                 if i < NY - 1:
                     grad_pair[k, half(at, h), :] = both.astype(BF16)
                     remote(
@@ -254,21 +268,21 @@
         unit = values * (1.0 / jnp.maximum(most, TINY))
         return most * jnp.sqrt(column(unit * unit))
 
+    def share_scale():
+        over_cells(lambda p: remote(inverse_mine, inverse.at[cell], scale_send_sem, scale_recv_sem, (dp, p)).start())
+
     def sum_start(k, rows):
-        sums_mine[k] = jnp.zeros((8, COLS), F32)
         for i, row in enumerate(rows):
-            sums_mine[k, pl.ds(i, 1), :] = row
+            sums_mine[k, pl.ds(i + 1, 1), :] = row
         mine = sums_mine.at[k]
         over_dp(
             lambda p: remote(mine, sums_dp.at[k, dp], small_send_sem.at[k, 0], small_recv_sem.at[k, 0], (p, cell)).start()
         )
         sums_dp[k, dp] = sums_mine[k]
 
-    def sum_middle(k, extra=None):
+    def sum_middle(k):
         wait_bytes(sums_dp.at[k, pl.ds(0, N_DP - 1)], small_recv_sem.at[k, 0])
         sums_mid[k] = jnp.sum(sums_dp[k], axis=0)
-        if extra is not None:
-            sums_mid[k, pl.ds(7, 1), :] = extra
         half = sums_mid.at[k]
         over_cells(
             lambda p: remote(
@@ -298,27 +312,28 @@
     pass_dp(0)
 
     apply(tiles, col_of, row_of, direction_full.at[0], [image_send.at[0], image_exact])
+    sums_mine[...] = jnp.zeros_like(sums_mine)
+    sums_mine[0, pl.ds(0, 1), :] = column(gradient[0] * gradient[0])
+    observed_size = size_of(observed[...])
     image = scatter_cells(0)
+    sum_start(0, [column(image * image)])
     residual_out[...] = image
 
-    first = gradient[0]
-    sum_start(0, [column(first * first), column(image * image)])
-    observed_size = size_of(observed[...])
     scale = jnp.clip(observed_size / jnp.maximum(size_of(image), TINY), 1e-18, 1e18)
     scale = jnp.where(observed_size > 0.0, scale, 1.0)
     residual_full[1, my_rows, :] = (observed[...] - scale * image).astype(BF16)
-    inverse = 1.0 / scale
-    gather_cells(1, lambda: sum_middle(0, inverse))
-    gamma, delta = sum_end(0, 2)
-    alpha = gamma / delta
+    inverse_mine[...] = 1.0 / scale
+    inverse[cell] = inverse_mine[...]
+    gather_cells(1, lambda: sum_middle(0), share_scale)
+    wait_bytes(inverse.at[pl.ds(0, N_CELL - 1)], scale_recv_sem)
 
     for c in range(N_CELL):
-        share = alpha * sums_cell[0, c, pl.ds(7, 1), :]
+        factor = inverse[c]
         for part in range(DROWS // 16):
             at = c * DROWS + part * 16
             old = residual_full[0, pl.ds(at, 16), :].astype(F32)
             new = residual_full[1, pl.ds(at, 16), :].astype(F32)
-            value = old + share * (new - old)
+            value = factor * (new - old)
             high = value.astype(BF16)
             into = pl.ds(at % BLOCK, 16)
             wide_pieces[at // BLOCK, into, pl.ds(0, COLS)] = high
@@ -327,21 +342,30 @@
         both = jnp.dot(tiles_t[slot], wide_pieces[row_of[0, 0, slot]], preferred_element_type=F32)
         prod[slot] = both[:, :COLS] + both[:, COLS:]
     place(col_of, [grad_send.at[1]])
-    pass_dp(1)
+    def alpha_now():
+        gamma, delta = sum_end(0, 2)
+        scalars[pl.ds(0, 1), :] = gamma
+        scalars[pl.ds(1, 1), :] = delta
+        return gamma / delta
+
+    pass_dp(1, alpha_now)
 
     apply(tiles, col_of, row_of, direction_full.at[1], [image_send.at[1], image_exact])
+    sums_mine[1, pl.ds(0, 1), :] = column(gradient[1] * gradient[1])
     update = scatter_cells(1)
     image = residual_out[...]
-    second = gradient[1]
-    sum_start(1, [column(second * second), column(update * update), column(update * image)])
+    sum_start(1, [column(update * update), column(update * image)])
     sum_middle(1)
     gamma_one, update_square, cross = sum_end(1, 3)
+    gamma, delta = scalars[pl.ds(0, 1), :], scalars[pl.ds(1, 1), :]
+    alpha = gamma / delta
     beta = gamma_one / gamma
     delta_one = update_square + beta * (2.0 * cross + beta * delta)
     alpha_one = gamma_one / delta_one
     first = gradient[0]
     model_out[...] = alpha * first + alpha_one * (gradient[1] + beta * first)
     residual_out[...] = observed[...] - alpha * image - alpha_one * (update + beta * image)
+    wait_bytes(inverse.at[pl.ds(0, N_CELL - 1)], scale_send_sem)
     wait_sends(0)
     wait_sends(1)
 
@@ -376,10 +400,16 @@
             pltpu.VMEM((2, TILE, COLS), BF16),
             pltpu.VMEM((2, NZ * DROWS, COLS), F32),
             pltpu.VMEM((2, NZ * DROWS, COLS), F32),
-            pltpu.VMEM((2, 8, COLS), F32),
-            pltpu.VMEM((2, N_DP, 8, COLS), F32),
-            pltpu.VMEM((2, 8, COLS), F32),
-            pltpu.VMEM((2, N_CELL, 8, COLS), F32),
+            pltpu.VMEM((2, 4, COLS), F32),
+            pltpu.VMEM((2, N_DP, 4, COLS), F32),
+            pltpu.VMEM((2, 4, COLS), F32),
+            pltpu.VMEM((2, N_CELL, 4, COLS), F32),
+            pltpu.VMEM((TILE // 2, COLS), F32),
+            pltpu.VMEM((1, COLS), F32),
+            pltpu.VMEM((N_CELL, 1, COLS), F32),
+            pltpu.VMEM((8, COLS), F32),
+            dma,
+            dma,
             dma,
             dma((2,)),
             dma((2, NZ)),

time: 105 us -> 103 us (0.981)
  Pallas kernels: 101 us -> 99.9 us
    pallas_call x1, Pallas kernels: 101 us -> 99.9 us  [shards(): pl.pallas_call(cgls, out_shape=(jax.ShapeDtypeStruct((CROWS, COLS), F32),...]
where the time goes in v6:
time: 103 us
  Pallas kernels  99.9 us (97%)
  local copies, waits for them, and re-layouts  2.04 us (2%)
  between operations  1.29 us (1%)
    pallas_call x1, Pallas kernels, shards(): pl.pallas_call(cgls, out_shape=(jax.ShapeDtypeStruct((CROWS, COLS), F32),...  99.9 us

profile of v6, /device:TPU:1, one launch (start us, length us, event | category | flops | bytes accessed | tf_op | source)
XLA Modules:
  0.0 103.2 jit_solution(8999909109709081856)
XLA Ops:
  1.3 99.9 %cgls.1 = (f32[96,128]{1,0:T(8,128)}, f32[48,128]{1,0:T(8,128)}) custom-call(bf16[8,256,256]{2,1,0:T(8,128)(2,1)} %bitcast.1, s32[1,1,8]{2,1,0:T(1,128)} %row_of.1, s32[1,1,8]{2,1,0:T(1,128)} %col_of.1, s32[1,1]{1,0:T(1,128)S(6)} %copy.9.counts, f32[48,128]{1,0:T(8,128)} %observed.1), custom_call_target="tpu_custom_call" | custom-call | tf_op jit(solution)/shard_map/cgls/pallas_call | solution.py:377
  101.2 0.0 copy-start
  101.2 1.4 %copy.10 = f32[96,128]{1,0:T(8,128)} copy(f32[96,128]{1,0:T(8,128)} %get-tuple-element.4) | data formatting | bytes 98304
  102.6 0.0 copy-done
  102.6 0.6 copy.11
Async XLA Ops:
  101.2 1.4 %copy-start = (f32[48,128]{1,0:T(8,128)S(1)}, f32[48,128]{1,0:T(8,128)}, u32[]{:S(2)}) copy-start(f32[48,128]{1,0:T(8,128)} %get-tuple-element.5) | copy-start | bytes 73732

commit v7 on v6

--- a/solution.py
+++ b/solution.py
@@ -141,31 +141,44 @@
         for slot in range(SLOTS):
             prod[slot] = jnp.dot(matrix[slot], pieces[source[0, 0, slot]], preferred_element_type=F32)
 
-    def apply(matrix, source, target, vector, sends):
+    def apply(matrix, source, target, vector, sends, after=None):
         for at in range(6):
             pieces[at] = vector[pl.ds(at * BLOCK, BLOCK), :]
         multiply(matrix, source)
-        place(target, sends)
-
-    def place(target, sends):
-        def one(at, carry):
+        place(target, sends, after)
+
+    def place(target, sends, after=None):
+        for at in range(6):
             total = jnp.zeros((BLOCK, COLS), F32)
             for slot in range(SLOTS):
                 here = jnp.logical_and(target[0, 0, slot] == at, slot < used)
                 total = total + here.astype(F32) * prod[slot]
             for send in sends:
-                send[rows_of(at, BLOCK), :] = total.astype(send.dtype)
-            return carry
-
-        lax.fori_loop(0, 6, one, 0)
-
-    def gather_cells(k, between=None, beside=None):
+                send[pl.ds(at * BLOCK, BLOCK), :] = total.astype(send.dtype)
+            if after is not None:
+                after(at)
+
+    def pair_copies(k):
+        def after(at):
+            for to in range(NY):
+                if at * BLOCK < (to + 1) * 2 * CROWS <= (at + 1) * BLOCK:
+                    remote(
+                        rows_at(grad_send.at[k], to * 2 + 1 - core, CROWS),
+                        pair_recv.at[k, pl.ds(to * CROWS, CROWS)],
+                        pair_send_sem.at[k],
+                        pair_recv_sem.at[k, to],
+                        sibling,
+                    ).start()
+
+        return after
+
+    def gather_cells(k, between=None, beside=None, arrived=None):
         full = residual_full.at[k]
         mine = full.at[my_rows]
         for i in range(NZ - 1):
             remote(mine, mine, gather_send_sem.at[k], gather_z_sem.at[k, z], (dp, z_at(i) * NX + x)).start()
         for i in range(NX - 1):
-            remote(mine, mine, gather_send_sem.at[k], gather_x_sem.at[k], (dp, z * NX + x_at(i))).start()
+            remote(mine, mine, gather_send_sem.at[k], gather_x_sem.at[k, z], (dp, z * NX + x_at(i))).start()
         if beside is not None:
             beside()
         for i in range(NZ - 1):
@@ -175,8 +188,12 @@
             slot = rows_at(full, src * NX + x, DROWS)
             wait_bytes(slot, gather_z_sem.at[k, src])
             for j in range(NX - 1):
-                remote(slot, slot, gather_send_sem.at[k], gather_x_sem.at[k], (dp, z * NX + x_at(j))).start()
-        wait_bytes(full.at[pl.ds(0, NZ * (NX - 1) * DROWS)], gather_x_sem.at[k])
+                remote(slot, slot, gather_send_sem.at[k], gather_x_sem.at[k, src], (dp, z * NX + x_at(j))).start()
+        for i in range(NZ):
+            src = z_at(NZ - 1 - i)
+            wait_bytes(full.at[pl.ds(0, (NX - 1) * DROWS)], gather_x_sem.at[k, src])
+            if arrived is not None:
+                arrived(i, src)
 
     def pass_dp(k, factor=None):
         full = direction_full.at[k]
@@ -184,10 +201,6 @@
         def half(index, h):
             return pl.ds(pl.multiple_of(index * CROWS + h * HALF, HALF), HALF)
 
-        for i in range(NY):
-            at = y_at(i)
-            src = rows_at(grad_send.at[k], at * 2 + 1 - core, CROWS)
-            remote(src, rows_at(pair_recv.at[k], at, CROWS), pair_send_sem.at[k], pair_recv_sem.at[k, at], sibling).start()
         if factor is not None:
             share = factor()
         totals = []
@@ -308,7 +321,7 @@
         wait_bytes(sums_cell.at[k, pl.ds(0, N_CELL - 1)], small_send_sem.at[k, 1])
 
     gather_cells(0)
-    apply(tiles_t, row_of, col_of, residual_full.at[0], [grad_send.at[0]])
+    apply(tiles_t, row_of, col_of, residual_full.at[0], [grad_send.at[0]], pair_copies(0))
     pass_dp(0)
 
     apply(tiles, col_of, row_of, direction_full.at[0], [image_send.at[0], image_exact])
@@ -324,24 +337,29 @@
     residual_full[1, my_rows, :] = (observed[...] - scale * image).astype(BF16)
     inverse_mine[...] = 1.0 / scale
     inverse[cell] = inverse_mine[...]
-    gather_cells(1, lambda: sum_middle(0), share_scale)
-    wait_bytes(inverse.at[pl.ds(0, N_CELL - 1)], scale_recv_sem)
-
-    for c in range(N_CELL):
-        factor = inverse[c]
-        for part in range(DROWS // 16):
-            at = c * DROWS + part * 16
-            old = residual_full[0, pl.ds(at, 16), :].astype(F32)
-            new = residual_full[1, pl.ds(at, 16), :].astype(F32)
-            value = factor * (new - old)
-            high = value.astype(BF16)
-            into = pl.ds(at % BLOCK, 16)
-            wide_pieces[at // BLOCK, into, pl.ds(0, COLS)] = high
-            wide_pieces[at // BLOCK, into, pl.ds(COLS, COLS)] = (value - high.astype(F32)).astype(BF16)
+
+    def change(i, src):
+        if i == 0:
+            wait_bytes(inverse.at[pl.ds(0, N_CELL - 1)], scale_recv_sem)
+        for j in range(NX):
+            c = src * NX + j
+            factor = inverse[c]
+            for part in range(DROWS // 16):
+                at = c * DROWS + part * 16
+                rows = pl.ds(pl.multiple_of(at, 16), 16)
+                old = residual_full[0, rows, :].astype(F32)
+                new = residual_full[1, rows, :].astype(F32)
+                value = factor * (new - old)
+                high = value.astype(BF16)
+                into = pl.ds(pl.multiple_of(at % BLOCK, 16), 16)
+                wide_pieces[at // BLOCK, into, pl.ds(0, COLS)] = high
+                wide_pieces[at // BLOCK, into, pl.ds(COLS, COLS)] = (value - high.astype(F32)).astype(BF16)
+
+    gather_cells(1, lambda: sum_middle(0), share_scale, change)
     for slot in range(SLOTS):
         both = jnp.dot(tiles_t[slot], wide_pieces[row_of[0, 0, slot]], preferred_element_type=F32)
         prod[slot] = both[:, :COLS] + both[:, COLS:]
-    place(col_of, [grad_send.at[1]])
+    place(col_of, [grad_send.at[1]], pair_copies(1))
     def alpha_now():
         gamma, delta = sum_end(0, 2)
         scalars[pl.ds(0, 1), :] = gamma
@@ -413,7 +431,7 @@
             dma,
             dma((2,)),
             dma((2, NZ)),
-            dma((2,)),
+            dma((2, NZ)),
             dma((2,)),
             dma((2, 2, NY)),
             dma((2,)),
@@ -430,7 +448,7 @@
             dma((2, 2)),
         ],
         compiler_params=pltpu.CompilerParams(
-            collective_id=0, has_side_effects=True, vmem_limit_bytes=60 * 1024 * 1024
+            collective_id=0, has_side_effects=True, vmem_limit_bytes=56_200_000
         ),
         name="cgls",
     )(blocks[0, 0], row_block, col_block, counts, observed)

time: 103 us -> 103 us (level)
    unnamed x4 -> x8, local copies, waits for them, and re-layouts: 2.04 us -> 2.62 us
where the time goes in v7:
time: 103 us
  Pallas kernels  99.1 us (96%)
  local copies, waits for them, and re-layouts  2.62 us (3%)
  between operations  1.3 us (1%)
    pallas_call x1, Pallas kernels, shards(): pl.pallas_call(cgls, out_shape=(jax.ShapeDtypeStruct((CROWS, COLS), F32),...  99.1 us
    unnamed x8, local copies, waits for them, and re-layouts  2.62 us

profile of v7, /device:TPU:1, one launch (start us, length us, event | category | flops | bytes accessed | tf_op | source)
XLA Modules:
  0.0 103.0 jit_solution(511347955492595860)
XLA Ops:
  1.3 0.0 copy-start.1
  1.3 0.0 copy-start.2
  1.3 0.6 copy-done.1
  1.9 0.0 copy-done.2
  1.9 0.0 copy-start
  2.0 0.7 copy-done
  2.7 99.1 %cgls.1 = (f32[96,128]{1,0:T(8,128)S(1)}, f32[48,128]{1,0:T(8,128)S(1)}) custom-call(bf16[8,256,256]{2,1,0:T(8,128)(2,1)} %bitcast.1, s32[1,1,8]{2,1,0:T(1,128)S(1)} %copy-done.1, s32[1,1,8]{2,1,0:T(1,128)S(1)} %copy-done.2, s32[1,1]{1,0:T(1,128)S(6)} %copy.9.counts, f32[48,128]{1,0:T(8,128)S(1)} %copy-done), custom_call_target="tpu_custom_call" | custom-call | tf_op jit(solution)/shard_map/cgls/pallas_call | solution.py:395
  101.8 0.6 copy.10
  102.4 0.6 copy.11
Async XLA Ops:
  1.3 0.7 copy-start.1
  1.3 0.7 copy-start.2
  1.9 0.7 copy-start
